TPU v7x, 32 devices: a whole 2x2x4 slice. The times are simulated.
32 devices in a mesh: section: 2 (over x), tok: 16 (over z, y, core).
Axes of the slice: x: 2, y: 2, z: 4, core: 2. Of those that a mesh axis runs over, the one named last changes fastest.
Arguments:
- inputs: bfloat16 [2, 1024, 1024], P(None, 'tok'), may hold values from -6 to 6
- cotangent: bfloat16 [2, 1024, 1024], P(None, 'tok'), may hold values from -6 to 6
- lengths: int32 [2, 8], replicated, may hold values from 1 to 1017, as said below
- prefix_keys: bfloat16 [2, 64, 1024], P('section'), may hold values from -6 to 6
- prefix_values: bfloat16 [2, 64, 1024], P('section'), may hold values from -6 to 6
- w_query: bfloat16 [2, 1024, 1024], P('section', 'tok'), may hold values from -0.1875 to 0.1875
- b_query: bfloat16 [2, 1024], P('section', 'tok'), may hold values from -3 to 3
- w_key: bfloat16 [2, 1024, 1024], P('section', 'tok'), may hold values from -0.1875 to 0.1875
- w_value: bfloat16 [2, 1024, 1024], P('section', 'tok'), may hold values from -0.1875 to 0.1875
- b_value: bfloat16 [2, 1024], P('section', 'tok'), may hold values from -3 to 3
- w_out: bfloat16 [2, 1024, 1024], P('section', 'tok'), may hold values from -6 to 6
- b_out: bfloat16 [2, 1024], P('section', 'tok'), may hold values from -6 to 6
- norm1_gain: bfloat16 [2, 1024], P('section', 'tok'), may hold values from 0.25 to 1.75
- norm1_shift: bfloat16 [2, 1024], P('section', 'tok'), may hold values from -3 to 3
- w_up: bfloat16 [2, 1024, 4096], P('section', 'tok'), may hold values from -0.1875 to 0.1875
- b_up: bfloat16 [2, 4096], P('section', 'tok'), may hold values from -3 to 3
- w_down: bfloat16 [2, 4096, 1024], P('section', 'tok'), may hold values from -0.09375 to 0.09375
- b_down: bfloat16 [2, 1024], P('section', 'tok'), may hold values from -3 to 3
- norm2_gain: bfloat16 [2, 1024], P('section', 'tok'), may hold values from 0.25 to 1.75
- norm2_shift: bfloat16 [2, 1024], P('section', 'tok'), may hold values from -3 to 3
Outputs:
- layer_outputs: bfloat16 [2, 2, 1024, 1024], P('section', None, 'tok')
- input_grads: bfloat16 [2, 2, 1024, 1024], P('section', None, 'tok')
- grad_w_query: float32 [2, 1024, 1024], P('section', 'tok')
- grad_b_query: float32 [2, 1024], P('section', 'tok')
- grad_w_key: float32 [2, 1024, 1024], P('section', 'tok')
- grad_w_value: float32 [2, 1024, 1024], P('section', 'tok')
- grad_b_value: float32 [2, 1024], P('section', 'tok')
- grad_w_out: float32 [2, 1024, 1024], P('section', 'tok')
- grad_b_out: float32 [2, 1024], P('section', 'tok')
- grad_norm1_gain: float32 [2, 1024], P('section', 'tok')
- grad_norm1_shift: float32 [2, 1024], P('section', 'tok')
- grad_w_up: float32 [2, 1024, 4096], P('section', 'tok')
- grad_b_up: float32 [2, 4096], P('section', 'tok')
- grad_w_down: float32 [2, 4096, 1024], P('section', 'tok')
- grad_b_down: float32 [2, 1024], P('section', 'tok')
- grad_norm2_gain: float32 [2, 1024], P('section', 'tok')
- grad_norm2_shift: float32 [2, 1024], P('section', 'tok')
- grad_prefix_keys: float32 [2, 64, 1024], P('section')
- grad_prefix_values: float32 [2, 64, 1024], P('section')
Inputs may be any that keep to these rules, and one draw needn't show every extreme that they name: In each micro-batch the 8 lengths sum to 1024; one document, at a position drawn per micro-batch, covers rows of the first and of the last 64 tokens.
All inputs are finite; a program needn't handle non-finite values.
Results may differ from a plain program's by a relative error of at most 0.028.
Values may be sent and summed in bfloat16 or wider, within the bound.
A program may use at most 256 MiB of HBM per device.

v0:
```python
import jax
import jax.numpy as jnp
from jax import lax
from jax.sharding import PartitionSpec as P

HEADS = 16
HEAD = 64


NEGATIVE = -1e30


def from_behind(block, axis, distance):
    devices = range(lax.axis_size(axis))
    route = [(i - distance, i) for i in devices if i - distance in devices]
    return lax.ppermute(block, axis, route)


def segment_of(lengths_row, positions):
    ends = jnp.cumsum(lengths_row, dtype=jnp.int32)
    return jnp.sum((positions[:, None] >= ends[None, :]).astype(jnp.int32), axis=1, dtype=jnp.int32)


def normalize(value, gain, shift):
    centred = value - jnp.mean(value, axis=-1, keepdims=True)
    spread = jnp.mean(centred * centred, axis=-1, keepdims=True)
    return centred * lax.rsqrt(spread + 1e-05) * gain + shift


def gelu_exact(value):
    return jax.nn.gelu(value, approximate=False)


def project(left, right):
    return jnp.dot(left, right, preferred_element_type=jnp.float32)


def project_back(left, weight):
    return jnp.einsum("tf,df->td", left, weight, preferred_element_type=jnp.float32)


def contract_rows(left, right):
    return jnp.einsum("tf,td->fd", left, right, preferred_element_type=jnp.float32)


def split_heads(value):
    return value.reshape(value.shape[0], HEADS, HEAD)


def in_blocks(step_fn, running, arrays, offset_row):
    total_rows = arrays[0].shape[0]
    block_rows = 1024 if total_rows > 1024 and total_rows % 1024 == 0 else total_rows
    if block_rows == total_rows:
        return step_fn(running, arrays, offset_row)
    stacked = tuple(
        (
            member.reshape((total_rows // block_rows, block_rows) + member.shape[1:])
            for member in arrays
        )
    )
    offsets = offset_row + block_rows * jnp.arange(total_rows // block_rows, dtype=jnp.int32)

    def scan_step(inner, packet):
        return (step_fn(inner, packet[0], packet[1]), None)

    result, unused = lax.scan(scan_step, running, (stacked, offsets))
    return result


def masked_scores(query_part, key_part, query_segment, key_segment):
    raw_scores = jnp.einsum(
        "qhe,khe->hqk",
        split_heads(query_part),
        split_heads(key_part),
        preferred_element_type=jnp.float32,
    ) * HEAD ** (-0.5)
    return jnp.where((query_segment[:, None] == key_segment[None, :])[None], raw_scores, NEGATIVE)


def prefix_scores(queries, prefix_key_rows):
    return jnp.einsum(
        "qhe,khe->hqk",
        split_heads(queries),
        split_heads(prefix_key_rows),
        preferred_element_type=jnp.float32,
    ) * HEAD ** (-0.5)


def gather_weights(shards):
    return (
        lax.all_gather(shards[0], "tok", axis=1, tiled=True),
        lax.all_gather(shards[1], "tok", axis=1, tiled=True),
        lax.all_gather(shards[2], "tok", axis=1, tiled=True),
        lax.all_gather(shards[3], "tok", axis=1, tiled=True),
        lax.all_gather(shards[4], "tok", axis=1, tiled=True),
        lax.all_gather(shards[5], "tok", axis=1, tiled=True),
        lax.all_gather(shards[6], "tok", axis=1, tiled=True),
        lax.all_gather(shards[7], "tok", axis=1, tiled=True),
        lax.all_gather(shards[8], "tok", axis=1, tiled=True),
        lax.all_gather(shards[9], "tok", axis=1, tiled=True),
        lax.all_gather(shards[10], "tok", axis=1, tiled=True),
        lax.all_gather(shards[11], "tok", axis=1, tiled=True),
        lax.all_gather(shards[12], "tok", axis=1, tiled=True),
        lax.all_gather(shards[13], "tok", axis=1, tiled=True),
        lax.all_gather(shards[14], "tok", axis=1, tiled=True),
    )


def front_part(inbound, weights):
    queries = (project(inbound, weights[0]) + weights[1].astype(jnp.float32)).astype(jnp.bfloat16)
    key_rows = project(inbound, weights[2]).astype(jnp.bfloat16)
    value_rows = (project(inbound, weights[3]) + weights[4].astype(jnp.float32)).astype(
        jnp.bfloat16
    )
    return (queries, key_rows, value_rows)


def attention_forward(
    queries, key_rows, value_rows, prefix_key_rows, prefix_value_rows, lengths_row, own_segment
):
    first_scores = prefix_scores(queries, prefix_key_rows)
    highest = jnp.max(first_scores, axis=2)
    denominator = jnp.sum(jnp.exp(first_scores - highest[..., None]), axis=2)

    def total_block(state, piece, offset_row):
        old_high, old_denominator = state
        key_part = piece[0]
        key_segment = segment_of(
            lengths_row, offset_row + jnp.arange(key_part.shape[0], dtype=jnp.int32)
        )
        raw_scores = masked_scores(queries, key_part, own_segment, key_segment)
        new_high = jnp.maximum(old_high, jnp.max(raw_scores, axis=2))
        new_denominator = old_denominator * jnp.exp(old_high - new_high) + jnp.sum(
            jnp.exp(raw_scores - new_high[..., None]), axis=2
        )
        return (new_high, new_denominator)

    highest, denominator = in_blocks(
        total_block,
        (highest, denominator),
        (lax.all_gather(key_rows, "tok", axis=0, tiled=True),),
        jnp.int32(0),
    )
    logsum = highest + jnp.log(denominator)
    summed = jnp.einsum(
        "hqk,khe->qhe",
        jnp.exp(first_scores - logsum[..., None]).astype(jnp.bfloat16),
        split_heads(prefix_value_rows),
        preferred_element_type=jnp.float32,
    )

    def absorb_block(running, piece, offset_row):
        key_part, value_part = piece
        key_segment = segment_of(
            lengths_row, offset_row + jnp.arange(key_part.shape[0], dtype=jnp.int32)
        )
        probs_part = jnp.exp(
            masked_scores(queries, key_part, own_segment, key_segment) - logsum[..., None]
        )
        return running + jnp.einsum(
            "hqk,khe->qhe",
            probs_part.astype(jnp.bfloat16),
            split_heads(value_part),
            preferred_element_type=jnp.float32,
        )

    summed = in_blocks(
        absorb_block,
        summed,
        (
            lax.all_gather(key_rows, "tok", axis=0, tiled=True),
            lax.all_gather(value_rows, "tok", axis=0, tiled=True),
        ),
        jnp.int32(0),
    )
    context = summed.reshape(queries.shape[0], -1)
    return (context, logsum)


def back_part(inbound, context, weights):
    context_low = context.astype(jnp.bfloat16)
    attended = project(context_low, weights[5]) + weights[6].astype(jnp.float32)
    normal_one, pull_one = jax.vjp(
        normalize,
        inbound.astype(jnp.float32) + attended,
        weights[7].astype(jnp.float32),
        weights[8].astype(jnp.float32),
    )
    normal_one_low = normal_one.astype(jnp.bfloat16)
    activation, pull_gelu = jax.vjp(
        gelu_exact, project(normal_one_low, weights[9]) + weights[10].astype(jnp.float32)
    )
    activation_low = activation.astype(jnp.bfloat16)
    mixed = project(activation_low, weights[11]) + weights[12].astype(jnp.float32)
    result, pull_two = jax.vjp(
        normalize,
        normal_one + mixed,
        weights[13].astype(jnp.float32),
        weights[14].astype(jnp.float32),
    )
    return (result, context_low, normal_one_low, pull_one, activation_low, pull_gelu, pull_two)


def query_backward(
    queries,
    d_context,
    logsum,
    delta,
    prefix_key_rows,
    prefix_value_rows,
    key_rows,
    value_rows,
    lengths_row,
    own_segment,
):
    context_heads = split_heads(d_context)
    query_heads = split_heads(queries)
    prefix_prob = jnp.exp(prefix_scores(queries, prefix_key_rows) - logsum[..., None])
    prefix_dprob = jnp.einsum(
        "qhe,khe->hqk",
        context_heads,
        split_heads(prefix_value_rows),
        preferred_element_type=jnp.float32,
    )
    prefix_dscore = (prefix_prob * (prefix_dprob - delta[..., None])).astype(jnp.bfloat16)
    grad_prefix_keys = jnp.einsum(
        "hqk,qhe->khe", prefix_dscore, query_heads, preferred_element_type=jnp.float32
    ) * HEAD ** (-0.5)
    grad_prefix_values = jnp.einsum(
        "hqk,qhe->khe",
        prefix_prob.astype(jnp.bfloat16),
        context_heads,
        preferred_element_type=jnp.float32,
    )
    grad_start = jnp.einsum(
        "hqk,khe->qhe",
        prefix_dscore,
        split_heads(prefix_key_rows),
        preferred_element_type=jnp.float32,
    )

    def pull_block(running, piece, offset_row):
        key_part, value_part = piece
        key_segment = segment_of(
            lengths_row, offset_row + jnp.arange(key_part.shape[0], dtype=jnp.int32)
        )
        probs_part = jnp.exp(
            masked_scores(queries, key_part, own_segment, key_segment) - logsum[..., None]
        )
        dprob = jnp.einsum(
            "qhe,khe->hqk",
            context_heads,
            split_heads(value_part),
            preferred_element_type=jnp.float32,
        )
        dscore = (probs_part * (dprob - delta[..., None])).astype(jnp.bfloat16)
        return running + jnp.einsum(
            "hqk,khe->qhe", dscore, split_heads(key_part), preferred_element_type=jnp.float32
        )

    grad_queries = in_blocks(
        pull_block,
        grad_start,
        (
            lax.all_gather(key_rows, "tok", axis=0, tiled=True),
            lax.all_gather(value_rows, "tok", axis=0, tiled=True),
        ),
        jnp.int32(0),
    )
    row_count = queries.shape[0]
    return (
        (grad_queries * HEAD ** (-0.5)).reshape(row_count, -1),
        grad_prefix_keys.reshape(prefix_key_rows.shape),
        grad_prefix_values.reshape(prefix_value_rows.shape),
    )


def key_backward(queries, d_context, logsum, delta, key_rows, value_rows, lengths_row, own_segment):
    all_logsum, all_delta = (
        lax.all_gather(logsum, "tok", axis=1, tiled=True),
        lax.all_gather(delta, "tok", axis=1, tiled=True),
    )
    value_heads = split_heads(value_rows)

    def spread_block(running, piece, offset_row):
        grad_keys, grad_values = running
        query_part, context_part = piece
        part_rows = query_part.shape[0]
        part_logsum = lax.dynamic_slice_in_dim(all_logsum, offset_row, part_rows, 1)
        part_delta = lax.dynamic_slice_in_dim(all_delta, offset_row, part_rows, 1)
        part_segment = segment_of(lengths_row, offset_row + jnp.arange(part_rows, dtype=jnp.int32))
        probs_part = jnp.exp(
            masked_scores(query_part, key_rows, part_segment, own_segment) - part_logsum[..., None]
        )
        context_heads = split_heads(context_part)
        dprob = jnp.einsum(
            "qhe,khe->hqk", context_heads, value_heads, preferred_element_type=jnp.float32
        )
        dscore = (probs_part * (dprob - part_delta[..., None])).astype(jnp.bfloat16)
        new_keys = grad_keys + jnp.einsum(
            "hqk,qhe->khe", dscore, split_heads(query_part), preferred_element_type=jnp.float32
        )
        new_values = grad_values + jnp.einsum(
            "hqk,qhe->khe",
            probs_part.astype(jnp.bfloat16),
            context_heads,
            preferred_element_type=jnp.float32,
        )
        return (new_keys, new_values)

    def spread(running, piece, offset_row):
        return in_blocks(spread_block, running, piece, offset_row)

    empty = jnp.zeros((key_rows.shape[0], HEADS, HEAD), jnp.float32)
    grad_keys, grad_values = spread(
        (empty, empty),
        (
            lax.all_gather(queries, "tok", axis=0, tiled=True),
            lax.all_gather(d_context, "tok", axis=0, tiled=True),
        ),
        jnp.int32(0),
    )
    row_count = key_rows.shape[0]
    return ((grad_keys * HEAD ** (-0.5)).reshape(row_count, -1), grad_values.reshape(row_count, -1))


def layer_backward(
    inbound, upstream, weights, prefix_key_rows, prefix_value_rows, lengths_row, own_segment
):
    queries, key_rows, value_rows = front_part(inbound, weights)
    context, logsum = attention_forward(
        queries, key_rows, value_rows, prefix_key_rows, prefix_value_rows, lengths_row, own_segment
    )
    result, context_low, normal_one_low, pull_one, activation_low, pull_gelu, pull_two = back_part(
        inbound, context, weights
    )
    d_sum, d_gain_two, d_shift_two = pull_two(upstream.astype(jnp.float32))
    d_mixed = d_sum.astype(jnp.bfloat16)
    grad_down = contract_rows(activation_low, d_mixed)
    grad_down_bias = jnp.sum(d_mixed.astype(jnp.float32), axis=0)
    (d_pre,) = pull_gelu(project_back(d_mixed, weights[11]))
    d_pre_low = d_pre.astype(jnp.bfloat16)
    grad_up = contract_rows(normal_one_low, d_pre_low)
    grad_up_bias = jnp.sum(d_pre_low.astype(jnp.float32), axis=0)
    d_resid, d_gain_one, d_shift_one = pull_one(d_sum + project_back(d_pre_low, weights[9]))
    d_attended = d_resid.astype(jnp.bfloat16)
    grad_out = contract_rows(context_low, d_attended)
    grad_out_bias = jnp.sum(d_attended.astype(jnp.float32), axis=0)
    d_context = project_back(d_attended, weights[5]).astype(jnp.bfloat16)
    delta = jnp.sum(split_heads(d_context).astype(jnp.float32) * split_heads(context), axis=2).T
    grad_queries, grad_prefix_keys, grad_prefix_values = query_backward(
        queries,
        d_context,
        logsum,
        delta,
        prefix_key_rows,
        prefix_value_rows,
        key_rows,
        value_rows,
        lengths_row,
        own_segment,
    )
    grad_keys, grad_values = key_backward(
        queries, d_context, logsum, delta, key_rows, value_rows, lengths_row, own_segment
    )
    queries_low = grad_queries.astype(jnp.bfloat16)
    keys_low = grad_keys.astype(jnp.bfloat16)
    values_low = grad_values.astype(jnp.bfloat16)
    grad_query_weight = contract_rows(inbound, queries_low)
    grad_query_bias = jnp.sum(queries_low.astype(jnp.float32), axis=0)
    grad_key_weight = contract_rows(inbound, keys_low)
    grad_value_weight = contract_rows(inbound, values_low)
    grad_value_bias = jnp.sum(values_low.astype(jnp.float32), axis=0)
    d_input = (
        d_resid
        + project_back(queries_low, weights[0])
        + project_back(keys_low, weights[2])
        + project_back(values_low, weights[3])
    )
    grads = (
        grad_query_weight,
        grad_query_bias,
        grad_key_weight,
        grad_value_weight,
        grad_value_bias,
        grad_out,
        grad_out_bias,
        d_gain_one,
        d_shift_one,
        grad_up,
        grad_up_bias,
        grad_down,
        grad_down_bias,
        d_gain_two,
        d_shift_two,
    )
    return (d_input, grads, (grad_prefix_keys, grad_prefix_values))


def sum_each(grads):
    return (
        lax.psum_scatter(grads[0][None], "tok", scatter_dimension=1, tiled=True),
        lax.psum_scatter(grads[1][None], "tok", scatter_dimension=1, tiled=True),
        lax.psum_scatter(grads[2][None], "tok", scatter_dimension=1, tiled=True),
        lax.psum_scatter(grads[3][None], "tok", scatter_dimension=1, tiled=True),
        lax.psum_scatter(grads[4][None], "tok", scatter_dimension=1, tiled=True),
        lax.psum_scatter(grads[5][None], "tok", scatter_dimension=1, tiled=True),
        lax.psum_scatter(grads[6][None], "tok", scatter_dimension=1, tiled=True),
        lax.psum_scatter(grads[7][None], "tok", scatter_dimension=1, tiled=True),
        lax.psum_scatter(grads[8][None], "tok", scatter_dimension=1, tiled=True),
        lax.psum_scatter(grads[9][None], "tok", scatter_dimension=1, tiled=True),
        lax.psum_scatter(grads[10][None], "tok", scatter_dimension=1, tiled=True),
        lax.psum_scatter(grads[11][None], "tok", scatter_dimension=1, tiled=True),
        lax.psum_scatter(grads[12][None], "tok", scatter_dimension=1, tiled=True),
        lax.psum_scatter(grads[13][None], "tok", scatter_dimension=1, tiled=True),
        lax.psum_scatter(grads[14][None], "tok", scatter_dimension=1, tiled=True),
    )


def by_section(listing, is_first, early_first):
    stacked = jnp.stack(listing)
    window_count = len(listing) - 1
    if early_first:
        return jnp.where(is_first, stacked[:window_count], stacked[1:])
    return jnp.where(is_first, stacked[1:], stacked[:window_count])


def local(
    inputs,
    cotangent,
    lengths,
    prefix_keys,
    prefix_values,
    w_query,
    b_query,
    w_key,
    w_value,
    b_value,
    w_out,
    b_out,
    norm1_gain,
    norm1_shift,
    w_up,
    b_up,
    w_down,
    b_down,
    norm2_gain,
    norm2_shift,
):
    micro_count = inputs.shape[0]
    tok_rows = inputs.shape[1]
    model_width = inputs.shape[2]
    section_index = lax.axis_index("section")
    is_first = section_index == 0
    own_positions = lax.axis_index("tok") * tok_rows + jnp.arange(tok_rows, dtype=jnp.int32)
    shard_list = (
        w_query,
        b_query,
        w_key,
        w_value,
        b_value,
        w_out,
        b_out,
        norm1_gain,
        norm1_shift,
        w_up,
        b_up,
        w_down,
        b_down,
        norm2_gain,
        norm2_shift,
    )
    prefix_key_rows = prefix_keys[0]
    prefix_value_rows = prefix_values[0]
    weights = tuple((member[0] for member in gather_weights(shard_list)))
    received = jnp.zeros((tok_rows, model_width), jnp.bfloat16)
    seen_inputs = []
    seen_outputs = []
    seen_context = []
    seen_logsum = []
    for moment in range(micro_count + 1):
        current = jnp.clip(moment - section_index, 0, micro_count - 1)
        lengths_row = lengths[current]
        own_segment = segment_of(lengths_row, own_positions)
        inbound = jnp.where(is_first, inputs[min(moment, micro_count - 1)], received)
        queries, key_rows, value_rows = front_part(inbound, weights)
        context, logsum = attention_forward(
            queries,
            key_rows,
            value_rows,
            prefix_key_rows,
            prefix_value_rows,
            lengths_row,
            own_segment,
        )
        result = back_part(inbound, context, weights)[0].astype(jnp.bfloat16)
        seen_inputs.append(inbound)
        seen_outputs.append(result)
        seen_context.append(context)
        seen_logsum.append(logsum)
        if moment < micro_count:
            received = from_behind(result, "section", 1)
    kept_inputs = by_section(seen_inputs, is_first, True)
    weights = tuple((member[0] for member in gather_weights(shard_list)))
    back_received = jnp.zeros((tok_rows, model_width), jnp.bfloat16)
    grad_shards = tuple((jnp.zeros(member.shape, jnp.float32) for member in shard_list))
    prefix_key_total = jnp.zeros(prefix_key_rows.shape, jnp.float32)
    prefix_value_total = jnp.zeros(prefix_value_rows.shape, jnp.float32)
    seen_grads = []
    for moment in range(micro_count + 1):
        current = moment - 1 + section_index
        is_valid = ((current >= 0) & (current < micro_count)).astype(jnp.float32)
        picked = jnp.clip(current, 0, micro_count - 1)
        lengths_row = lengths[picked]
        own_segment = segment_of(lengths_row, own_positions)
        upstream = jnp.where(is_first, back_received, cotangent[min(moment, micro_count - 1)])
        d_input, grads, prefix_grads = layer_backward(
            kept_inputs[picked],
            upstream,
            weights,
            prefix_key_rows,
            prefix_value_rows,
            lengths_row,
            own_segment,
        )
        d_input_low = d_input.astype(jnp.bfloat16)
        seen_grads.append(d_input_low)
        if moment < micro_count:
            back_received = from_behind(d_input_low, "section", -1)
        grads = tuple((member * is_valid for member in grads))
        prefix_key_total = prefix_key_total + prefix_grads[0] * is_valid
        prefix_value_total = prefix_value_total + prefix_grads[1] * is_valid
        scattered = sum_each(grads)
        grad_shards = tuple((older + newer for older, newer in zip(grad_shards, scattered)))
    layer_outputs = by_section(seen_outputs, is_first, True)[None]
    input_grads = by_section(seen_grads, is_first, False)[None]
    prefix_sums = lax.psum((prefix_key_total, prefix_value_total), "tok")
    return (
        layer_outputs,
        input_grads,
        grad_shards[0],
        grad_shards[1],
        grad_shards[2],
        grad_shards[3],
        grad_shards[4],
        grad_shards[5],
        grad_shards[6],
        grad_shards[7],
        grad_shards[8],
        grad_shards[9],
        grad_shards[10],
        grad_shards[11],
        grad_shards[12],
        grad_shards[13],
        grad_shards[14],
        prefix_sums[0][None],
        prefix_sums[1][None],
    )


def solution(mesh):
    placed = (
        P(None, "tok", None),
        P(None, "tok", None),
        P(),
        P("section", None, None),
        P("section", None, None),
        P("section", "tok", None),
        P("section", "tok"),
        P("section", "tok", None),
        P("section", "tok", None),
        P("section", "tok"),
        P("section", "tok", None),
        P("section", "tok"),
        P("section", "tok"),
        P("section", "tok"),
        P("section", "tok", None),
        P("section", "tok"),
        P("section", "tok", None),
        P("section", "tok"),
        P("section", "tok"),
        P("section", "tok"),
    )
    return jax.shard_map(
        local,
        mesh=mesh,
        in_specs=placed,
        out_specs=(
            P("section", None, "tok", None),
            P("section", None, "tok", None),
            P("section", "tok", None),
            P("section", "tok"),
            P("section", "tok", None),
            P("section", "tok", None),
            P("section", "tok"),
            P("section", "tok", None),
            P("section", "tok"),
            P("section", "tok"),
            P("section", "tok"),
            P("section", "tok", None),
            P("section", "tok"),
            P("section", "tok", None),
            P("section", "tok"),
            P("section", "tok"),
            P("section", "tok"),
            P("section", None, None),
            P("section", None, None),
        ),
        check_vma=False,
    )
```

profile of v0, /device:TPU:0, one launch (start us, length us, event | category | flops | bytes accessed | tf_op | source)
XLA Modules:
  0.0 2477.7 jit_solution(9327804393654378886)
XLA Ops:
  10.4 43.9 %all-gather.33.cloned.1.call-done = bf16[1,1024,1024]{2,1,0:T(8,128)(2,1)} async-done(((bf16[1,64,1024]{2,1,0:T(8,128)(2,1)}), bf16[1,1024,1024]{2,1,0:T(8,128)(2,1)}) %all-gather.33.cloned.1.call-update) | async-done | bytes 2097168 | tf_op jit(solution)/shard_map/all_gather | solution.py:93
  65.8 59.9 %all-reduce.9 = (bf16[1024]{0:T(1024)(128)(2,1)S(1)}, bf16[1024]{0:T(1024)(128)(2,1)S(1)}, bf16[1024]{0:T(1024)(128)(2,1)S(1)}, bf16[1024]{0:T(1024)(128)(2,1)S(...) all-reduce(bf16[1024]{0:T(1024)(128)(2,1)S(1)} %dynamic-update-slic, ...), channel_id=1, replica_groups=mesh['section'=2,'tok'=16] {'tok'}, use_global_device_ids=true, to_apply=%add.1 | all-reduce | flops 8192 | bytes 32768
  132.1 17.3 all_gather.155
  153.4 28.9 %all-gather.35.cloned.1.call-done = bf16[1024,1024]{1,0:T(8,128)(2,1)} async-done(((bf16[64,1024]{1,0:T(8,128)(2,1)}), bf16[1024,1024]{1,0:T(8,128)(2,1)}) %all-gather.35.cloned.1.call-update) | async-done | bytes 2097168 | tf_op jit(solution)/shard_map/all_gather | solution.py:141
  189.0 36.0 %all-gather.39.cloned.1.call-done = bf16[1024,1024]{1,0:T(8,128)(2,1)} async-done(((bf16[64,1024]{1,0:T(8,128)(2,1)}), bf16[1024,1024]{1,0:T(8,128)(2,1)}) %all-gather.39.cloned.1.call-update) | async-done | bytes 2097168 | tf_op jit(solution)/shard_map/all_gather | solution.py:172
  233.2 34.0 %all-gather.41.cloned.1.call-done = bf16[1,1024,1024]{2,1,0:T(8,128)(2,1)} async-done(((bf16[1,64,1024]{2,1,0:T(8,128)(2,1)}), bf16[1,1024,1024]{2,1,0:T(8,128)(2,1)}) %all-gather.41.cloned.1.call-update) | async-done | bytes 2097168 | tf_op jit(solution)/shard_map/all_gather | solution.py:96
  269.7 73.5 %all-gather.43.cloned.1.call-done = bf16[1,1024,4096]{2,1,0:T(8,128)(2,1)} async-done(((bf16[1,64,4096]{2,1,0:T(8,128)(2,1)}), bf16[1,1024,4096]{2,1,0:T(8,128)(2,1)}) %all-gather.43.cloned.1.call-update) | async-done | bytes 8388624 | tf_op jit(solution)/shard_map/all_gather | solution.py:100
  343.1 75.3 %all-gather.45.cloned.1.call-done = bf16[1,4096,1024]{2,1,0:T(8,128)(2,1)} async-done(((bf16[1,256,1024]{2,1,0:T(8,128)(2,1)}), bf16[1,4096,1024]{2,1,0:T(8,128)(2,1)}) %all-gather.45.cloned.1.call-update) | async-done | bytes 8388624 | tf_op jit(solution)/shard_map/all_gather | solution.py:102
  418.5 11.3 fusion.953
  447.6 31.1 %all-gather.47.cloned.1.call-done = bf16[1024,1024]{1,0:T(8,128)(2,1)} async-done(((bf16[64,1024]{1,0:T(8,128)(2,1)}), bf16[1024,1024]{1,0:T(8,128)(2,1)}) %all-gather.47.cloned.1.call-update) | async-done | bytes 2097168 | tf_op jit(solution)/shard_map/all_gather | solution.py:141
  488.4 33.1 %all-gather.49.cloned.1.call-done = bf16[1024,1024]{1,0:T(8,128)(2,1)} async-done(((bf16[64,1024]{1,0:T(8,128)(2,1)}), bf16[1024,1024]{1,0:T(8,128)(2,1)}) %all-gather.49.cloned.1.call-update) | async-done | bytes 2097168 | tf_op jit(solution)/shard_map/all_gather | solution.py:172
  532.6 11.2 fusion.960
  568.5 25.7 %all-gather.55.cloned.1.call-done = bf16[1024,1024]{1,0:T(8,128)(2,1)} async-done(((bf16[64,1024]{1,0:T(8,128)(2,1)}), bf16[1024,1024]{1,0:T(8,128)(2,1)}) %all-gather.55.cloned.1.call-update) | async-done | bytes 2097168 | tf_op jit(solution)/shard_map/all_gather | solution.py:141
  604.4 32.6 %all-gather.57.cloned.1.call-done = bf16[1024,1024]{1,0:T(8,128)(2,1)} async-done(((bf16[64,1024]{1,0:T(8,128)(2,1)}), bf16[1024,1024]{1,0:T(8,128)(2,1)}) %all-gather.57.cloned.1.call-update) | async-done | bytes 2097168 | tf_op jit(solution)/shard_map/all_gather | solution.py:172
  647.2 5.6 fusion.45
  658.4 5.2 convert_reduce_fusion.2
  700.4 6.4 fusion.197
  711.5 20.1 all-gather.1
  733.9 18.1 all-gather
  775.8 5.2 fusion.48
  795.0 11.1 all-gather.61.cloned.1.call-done
  810.1 5.3 convert_reduce_fusion.5
  815.4 6.3 fusion.255
  835.8 6.2 collective-permute-done.2
  843.8 8.7 convert_reduce_fusion.1
  911.5 12.1 fusion.979
  925.4 19.6 all-gather.2
  957.1 17.9 all-gather.73.cloned.1.call-done
  985.8 5.2 fusion.51
  995.4 22.1 all-gather.67.cloned.1.call-done
  1030.8 6.5 fusion.196
  1042.0 20.0 all-gather.3
  1067.7 5.4 convert_reduce_fusion.4
  1073.1 6.2 fusion.254
  1092.4 6.1 collective-permute-done.3
  1101.0 8.7 convert_reduce_fusion
  1121.0 18.2 all-gather.4
  1168.3 6.4 fusion.195
  1197.5 4.7 convert_reduce_fusion.3
  1211.0 6.4 add_bitcast_fusion.2
  1224.1 6.4 add_bitcast_fusion.5
  1237.3 6.4 add_bitcast_fusion.3
  1250.3 19.5 all-gather.5
  1270.0 5.4 fusion.253
  1275.8 6.4 add_bitcast_fusion.4
  1283.5 8.9 fusion.943
  1292.4 8.0 fusion.944
  1300.5 19.2 add_bitcast_fusion
  1320.8 8.9 fusion.940
  1329.7 8.2 fusion.937
  1337.9 18.8 add_bitcast_fusion.1
  1363.2 41.1 %reduce-scatter.54.cloned.1.call-done = f32[64,1]{1,0:T(8,128)} async-done(((f32[1024,1]{1,0:T(8,128)}), f32[64,1]{1,0:T(8,128)}) %reduce-scatter.54.cloned.1.call-update) | async-done | bytes 272
  1405.7 57.0 %reduce-scatter.50.cloned.1.call-done = f32[64,1]{1,0:T(8,128)} async-done(((f32[1024,1]{1,0:T(8,128)}), f32[64,1]{1,0:T(8,128)}) %reduce-scatter.50.cloned.1.call-update) | async-done | bytes 272
  1464.1 57.3 %reduce-scatter.62.cloned.1.call-done = f32[64,1]{1,0:T(8,128)} async-done(((f32[1024,1]{1,0:T(8,128)}), f32[64,1]{1,0:T(8,128)}) %reduce-scatter.62.cloned.1.call-update) | async-done | bytes 272
  1522.7 57.0 %reduce-scatter.46.cloned.1.call-done = f32[64,1]{1,0:T(8,128)} async-done(((f32[1024,1]{1,0:T(8,128)}), f32[64,1]{1,0:T(8,128)}) %reduce-scatter.46.cloned.1.call-update) | async-done | bytes 272
  1581.1 63.5 %reduce-scatter.56.cloned.1.call-done = f32[256,1]{1,0:T(8,128)} async-done(((f32[4096,1]{1,0:T(8,128)}), f32[256,1]{1,0:T(8,128)}) %reduce-scatter.56.cloned.1.call-update) | async-done | bytes 1040
  1652.0 50.9 %reduce-scatter.48.cloned.1.call-done = f32[64,1]{1,0:T(8,128)} async-done(((f32[1024,1]{1,0:T(8,128)}), f32[64,1]{1,0:T(8,128)}) %reduce-scatter.48.cloned.1.call-update) | async-done | bytes 272
  1704.2 91.7 %all-reduce.12.cloned.1.call-done = (f32[1,64,1024]{2,1,0:T(8,128)}, f32[1,64,1024]{2,1,0:T(8,128)}) async-done(((f32[1,64,1024]{2,1,0:T(8,128)}, f32[1,64,1024]{2,1,0:T(8,128)}), (f32[1,64,1024]{2,1,0:T(8,128)}, f32[1,64,1024]{2,1,0:T(8,128)})) %all-reduce.12.cloned.1.call-update) | async-done | bytes 524304 | tf_op jit(solution)/shard_map/psum | solution.py:537
  1795.9 77.8 %reduce-scatter.40.cloned.1.call-done = f32[1,64,1024]{2,1,0:T(8,128)} async-done(((f32[1,1024,1024]{2,1,0:T(8,128)}), f32[1,64,1024]{2,1,0:T(8,128)}) %reduce-scatter.40.cloned.1.call-update) | async-done | bytes 262160 | tf_op jit(solution)/shard_map/reduce_scatter | solution.py:407
  1873.7 75.9 %reduce-scatter.34.cloned.1.call-done = f32[1,64,1024]{2,1,0:T(8,128)} async-done(((f32[1,1024,1024]{2,1,0:T(8,128)}), f32[1,64,1024]{2,1,0:T(8,128)}) %reduce-scatter.34.cloned.1.call-update) | async-done | bytes 262160 | tf_op jit(solution)/shard_map/reduce_scatter | solution.py:402
  1949.5 76.2 %reduce-scatter.38.cloned.1.call-done = f32[1,64,1024]{2,1,0:T(8,128)} async-done(((f32[1,1024,1024]{2,1,0:T(8,128)}), f32[1,64,1024]{2,1,0:T(8,128)}) %reduce-scatter.38.cloned.1.call-update) | async-done | bytes 262160 | tf_op jit(solution)/shard_map/reduce_scatter | solution.py:405
  2025.7 76.0 %reduce-scatter.36.cloned.1.call-done = f32[1,64,1024]{2,1,0:T(8,128)} async-done(((f32[1,1024,1024]{2,1,0:T(8,128)}), f32[1,64,1024]{2,1,0:T(8,128)}) %reduce-scatter.36.cloned.1.call-update) | async-done | bytes 262160 | tf_op jit(solution)/shard_map/reduce_scatter | solution.py:404
  2101.7 182.7 %reduce-scatter.44.cloned.1.call-done = f32[1,256,1024]{2,1,0:T(8,128)} async-done(((f32[1,4096,1024]{2,1,0:T(8,128)}), f32[1,256,1024]{2,1,0:T(8,128)}) %reduce-scatter.44.cloned.1.call-update) | async-done | bytes 1048592 | tf_op jit(solution)/shard_map/reduce_scatter | solution.py:413
  2284.4 182.8 %reduce-scatter.42.cloned.1.call-done = f32[1,64,4096]{2,1,0:T(8,128)} async-done(((f32[1,1024,4096]{2,1,0:T(8,128)}), f32[1,64,4096]{2,1,0:T(8,128)}) %reduce-scatter.42.cloned.1.call-update) | async-done | bytes 1048592 | tf_op jit(solution)/shard_map/reduce_scatter | solution.py:411
  (897 shorter events, 475.8 us)
Async XLA Ops:
  7.2 123.4 %copy-start.173 = (s32[2,8]{1,0:T(2,128)S(1)}, s32[2,8]{1,0:T(2,128)}, u32[]{:S(2)}) copy-start(s32[2,8]{1,0:T(2,128)} %param.22) | copy-start | bytes 196
  7.2 124.5 %copy-start.133 = (bf16[1,64,1024]{2,1,0:T(8,128)(2,1)S(1)}, bf16[1,64,1024]{2,1,0:T(8,128)(2,1)}, u32[]{:S(2)}) copy-start(bf16[1,64,1024]{2,1,0:T(8,128)(2,1)} %param.23) | copy-start | bytes 393220
  7.2 124.7 %copy-start.134 = (bf16[1,64,1024]{2,1,0:T(8,128)(2,1)S(1)}, bf16[1,64,1024]{2,1,0:T(8,128)(2,1)}, u32[]{:S(2)}) copy-start(bf16[1,64,1024]{2,1,0:T(8,128)(2,1)} %param.24) | copy-start | bytes 393220
  7.2 124.9 %copy-start.205 = (bf16[1,256]{1,0:T(2,128)(2,1)S(1)}, bf16[1,256]{1,0:T(2,128)(2,1)}, u32[]{:S(2)}) copy-start(bf16[1,256]{1,0:T(2,128)(2,1)} %param.35) | copy-start | bytes 1540
  7.2 47.1 %all-gather.33.cloned.1.call-start = ((), (), s32[]{:S(2)}) async-start(), calls=%async_computation.16 | async-start | bytes 2228224 | tf_op jit(solution)/shard_map/all_gather | solution.py:93
  8.0 117.7 %all-gather.37.cloned.1.call-start = ((), (), s32[]{:S(2)}) async-start(), calls=%async_computation.18 | async-start | bytes 2228224 | tf_op jit(solution)/shard_map/all_gather | solution.py:94
  8.7 141.7 %all-gather.31.cloned.1.call-start = ((), (), s32[]{:S(2)}) async-start(), calls=%async_computation.15 | async-start | bytes 2228224 | tf_op jit(solution)/shard_map/all_gather | solution.py:91
  9.4 172.8 %all-gather.35.cloned.1.call-start = ((), (), s32[]{:S(2)}) async-start(), calls=%async_computation.17 | async-start | bytes 2228224 | tf_op jit(solution)/shard_map/all_gather | solution.py:141
  10.4 256.8 %copy-start.29 = (bf16[1,64,1024]{2,1,0:T(8,128)(2,1)}, bf16[1,64,1024]{2,1,0:T(8,128)(2,1)S(1)}, u32[]{:S(2)}) copy-start(bf16[1,64,1024]{2,1,0:T(8,128)(2,1)S(1)} %slice_select_fusion.1) | copy-start | bytes 393220
  57.1 167.9 %all-gather.39.cloned.1.call-start = ((), (), s32[]{:S(2)}) async-start(), calls=%async_computation.19 | async-start | bytes 2228224 | tf_op jit(solution)/shard_map/all_gather | solution.py:172
  125.6 312.3 %copy-start.122 = (f32[1024]{0:T(1024)}, f32[1024]{0:T(1024)S(1)}, u32[]{:S(2)}) copy-start(f32[1024]{0:T(1024)S(1)} %add.1050) | copy-start | bytes 12292
  128.4 138.8 %all-gather.41.cloned.1.call-start = ((), (), s32[]{:S(2)}) async-start(), calls=%async_computation.20 | async-start | bytes 2228224 | tf_op jit(solution)/shard_map/all_gather | solution.py:96
  129.0 214.1 %all-gather.43.cloned.1.call-start = ((), (), s32[]{:S(2)}) async-start(), calls=%async_computation.21 | async-start | bytes 8912896 | tf_op jit(solution)/shard_map/all_gather | solution.py:100
  129.7 288.7 %all-gather.45.cloned.1.call-start = ((), (), s32[]{:S(2)}) async-start(), calls=%async_computation.22 | async-start | bytes 8912896 | tf_op jit(solution)/shard_map/all_gather | solution.py:102
  130.5 348.2 %all-gather.47.cloned.1.call-start = ((), (), s32[]{:S(2)}) async-start(), calls=%async_computation.23 | async-start | bytes 2228224 | tf_op jit(solution)/shard_map/all_gather | solution.py:141
  131.0 54.2 %copy-start.195 = (s32[8,1]{0,1:T(1,128)}, s32[8,1]{0,1:T(1,128)S(1)}, u32[]{:S(2)}) copy-start(s32[8,1]{0,1:T(1,128)S(1)} %reduce-window.50) | copy-start | bytes 100
  131.1 54.0 %copy-start.198 = (s32[8,1]{0,1:T(1,128)}, s32[8,1]{0,1:T(1,128)S(1)}, u32[]{:S(2)}) copy-start(s32[8,1]{0,1:T(1,128)S(1)} %reduce-window.51) | copy-start | bytes 100
  131.5 53.6 %copy-start.197 = (s32[8,1]{0,1:T(1,128)}, s32[8,1]{0,1:T(1,128)S(1)}, u32[]{:S(2)}) copy-start(s32[8,1]{0,1:T(1,128)S(1)} %reduce-window.52) | copy-start | bytes 100
  131.7 53.5 %copy-start.196 = (s32[8,1]{0,1:T(1,128)}, s32[8,1]{0,1:T(1,128)S(1)}, u32[]{:S(2)}) copy-start(s32[8,1]{0,1:T(1,128)S(1)} %reduce-window.53) | copy-start | bytes 100
  131.7 310.2 %copy-start.120 = (f32[1024]{0:T(1024)}, f32[1024]{0:T(1024)S(1)}, u32[]{:S(2)}) copy-start(f32[1024]{0:T(1024)S(1)} %add.1049) | copy-start | bytes 12292
  132.1 286.3 %copy-start.185 = (f32[1024]{0:T(1024)}, f32[1024]{0:T(1024)S(1)}, u32[]{:S(2)}) copy-start(f32[1024]{0:T(1024)S(1)} %add.1053) | copy-start | bytes 12292
  149.5 269.0 %copy-start.110 = (f32[1,4096]{1,0:T(1,128)}, f32[1,4096]{1,0:T(1,128)S(1)}, u32[]{:S(2)}) copy-start(f32[1,4096]{1,0:T(1,128)S(1)} %add.970) | copy-start | bytes 49156
  149.5 280.4 %copy-start.124 = (f32[1024]{0:T(1024)}, f32[1024]{0:T(1024)S(1)}, u32[]{:S(2)}) copy-start(f32[1024]{0:T(1024)S(1)} %add.1054) | copy-start | bytes 12292
  430.1 6.5 collective-permute-start
  437.9 83.6 %all-gather.49.cloned.1.call-start = ((), (), s32[]{:S(2)}) async-start(), calls=%async_computation.24 | async-start | bytes 2228224 | tf_op jit(solution)/shard_map/all_gather | solution.py:172
  440.7 153.5 %all-gather.55.cloned.1.call-start = ((), (), s32[]{:S(2)}) async-start(), calls=%async_computation.27 | async-start | bytes 2228224 | tf_op jit(solution)/shard_map/all_gather | solution.py:141
  544.1 6.5 collective-permute-start.1
  552.8 84.1 %all-gather.57.cloned.1.call-start = ((), (), s32[]{:S(2)}) async-start(), calls=%async_computation.28 | async-start | bytes 2228224 | tf_op jit(solution)/shard_map/all_gather | solution.py:172
  555.6 198.7 %all-gather.63.cloned.1.call-start = ((), (), s32[]{:S(2)}) async-start(), calls=%async_computation.31 | async-start | bytes 2228224 | tf_op jit(solution)/shard_map/all_gather | solution.py:141
  556.9 208.1 %all-gather.65.cloned.1.call-start = ((), (), s32[]{:S(2)}) async-start(), calls=%async_computation.32 | async-start | bytes 2228224 | tf_op jit(solution)/shard_map/all_gather | solution.py:172
  559.8 226.0 %all-gather.59.cloned.1.call-start = ((), (), s32[]{:S(2)}) async-start(), calls=%async_computation.29 | async-start | bytes 2228224 | tf_op jit(solution)/shard_map/all_gather | solution.py:318
  567.0 239.0 %all-gather.61.cloned.1.call-start = ((), (), s32[]{:S(2)}) async-start(), calls=%async_computation.30 | async-start | bytes 2228224 | tf_op jit(solution)/shard_map/all_gather | solution.py:319
  670.7 216.2 %all-gather.51.cloned.1.call-start = ((), (), s32[]{:S(2)}) async-start(), calls=%async_computation.25 | async-start | bytes 2228224 | tf_op jit(solution)/shard_map/all_gather | solution.py:141
  671.9 225.4 %all-gather.53.cloned.1.call-start = ((), (), s32[]{:S(2)}) async-start(), calls=%async_computation.26 | async-start | bytes 2228224 | tf_op jit(solution)/shard_map/all_gather | solution.py:172
  674.7 272.6 %all-gather.71.cloned.1.call-start = ((), (), s32[]{:S(2)}) async-start(), calls=%async_computation.35 | async-start | bytes 2228224 | tf_op jit(solution)/shard_map/all_gather | solution.py:141
  675.9 299.1 %all-gather.73.cloned.1.call-start = ((), (), s32[]{:S(2)}) async-start(), calls=%async_computation.36 | async-start | bytes 2228224 | tf_op jit(solution)/shard_map/all_gather | solution.py:172
  678.8 338.7 %all-gather.67.cloned.1.call-start = ((), (), s32[]{:S(2)}) async-start(), calls=%async_computation.33 | async-start | bytes 2228224 | tf_op jit(solution)/shard_map/all_gather | solution.py:318
  693.1 370.6 %all-gather.69.cloned.1.call-start = ((), (), s32[]{:S(2)}) async-start(), calls=%async_computation.34 | async-start | bytes 2228224 | tf_op jit(solution)/shard_map/all_gather | solution.py:319
  834.4 7.7 collective-permute-start.2
  859.6 281.9 %all-gather.75.cloned.1.call-start = ((), (), s32[]{:S(2)}) async-start(), calls=%async_computation.37 | async-start | bytes 2228224 | tf_op jit(solution)/shard_map/all_gather | solution.py:318
  883.2 310.3 %all-gather.77.cloned.1.call-start = ((), (), s32[]{:S(2)}) async-start(), calls=%async_computation.38 | async-start | bytes 2228224 | tf_op jit(solution)/shard_map/all_gather | solution.py:319
  1090.9 7.6 collective-permute-start.3
  1116.1 243.1 %reduce-scatter.58.cloned.1.call-start = ((), (), s32[]{:S(2)}) async-start(), calls=%async_computation.51 | async-start | bytes 557056
  1174.8 185.8 %reduce-scatter.60.cloned.1.call-start = ((), (), s32[]{:S(2)}) async-start(), calls=%async_computation.52 | async-start | bytes 557056
  1177.9 184.0 %reduce-scatter.52.cloned.1.call-start = ((), (), s32[]{:S(2)}) async-start(), calls=%async_computation.48 | async-start | bytes 557056
  1181.0 223.4 %reduce-scatter.54.cloned.1.call-start = ((), (), s32[]{:S(2)}) async-start(), calls=%async_computation.49 | async-start | bytes 557056
  1184.7 278.0 %reduce-scatter.50.cloned.1.call-start = ((), (), s32[]{:S(2)}) async-start(), calls=%async_computation.47 | async-start | bytes 557056
  1186.5 334.9 %reduce-scatter.62.cloned.1.call-start = ((), (), s32[]{:S(2)}) async-start(), calls=%async_computation.53 | async-start | bytes 557056
  1188.4 391.4 %reduce-scatter.46.cloned.1.call-start = ((), (), s32[]{:S(2)}) async-start(), calls=%async_computation.45 | async-start | bytes 557056
  1191.2 453.4 %reduce-scatter.56.cloned.1.call-start = ((), (), s32[]{:S(2)}) async-start(), calls=%async_computation.50 | async-start | bytes 2228224
  1193.4 509.5 %reduce-scatter.48.cloned.1.call-start = ((), (), s32[]{:S(2)}) async-start(), calls=%async_computation.46 | async-start | bytes 557056
  1204.8 591.0 %all-reduce.12.cloned.1.call-start = ((), (), s32[]{:S(2)}) async-start(), calls=%async_computation.54 | async-start | bytes 1048576 | tf_op jit(solution)/shard_map/psum | solution.py:537
  1210.9 662.7 %reduce-scatter.40.cloned.1.call-start = ((), (), s32[]{:S(2)}) async-start(), calls=%async_computation.42 | async-start | bytes 4456448 | tf_op jit(solution)/shard_map/reduce_scatter | solution.py:407
  1217.4 732.1 %reduce-scatter.34.cloned.1.call-start = ((), (), s32[]{:S(2)}) async-start(), calls=%async_computation.39 | async-start | bytes 4456448 | tf_op jit(solution)/shard_map/reduce_scatter | solution.py:402
  1230.6 795.1 %reduce-scatter.38.cloned.1.call-start = ((), (), s32[]{:S(2)}) async-start(), calls=%async_computation.41 | async-start | bytes 4456448 | tf_op jit(solution)/shard_map/reduce_scatter | solution.py:405
  1243.7 858.0 %reduce-scatter.36.cloned.1.call-start = ((), (), s32[]{:S(2)}) async-start(), calls=%async_computation.40 | async-start | bytes 4456448 | tf_op jit(solution)/shard_map/reduce_scatter | solution.py:404
  1282.2 1002.1 %reduce-scatter.44.cloned.1.call-start = ((), (), s32[]{:S(2)}) async-start(), calls=%async_computation.44 | async-start | bytes 17825792 | tf_op jit(solution)/shard_map/reduce_scatter | solution.py:413
  1319.7 1147.5 %reduce-scatter.42.cloned.1.call-start = ((), (), s32[]{:S(2)}) async-start(), calls=%async_computation.43 | async-start | bytes 17825792 | tf_op jit(solution)/shard_map/reduce_scatter | solution.py:411
  1357.7 291.6 %copy-start.56 = (f32[64,1024]{1,0:T(8,128)S(1)}, f32[64,1024]{1,0:T(8,128)}, u32[]{:S(2)}) copy-start(f32[64,1024]{1,0:T(8,128)} %copy-done.55) | copy-start | bytes 786436
  1358.4 290.9 %copy-start.201 = (f32[64]{0:T(128)S(1)}, f32[64]{0:T(128)}, u32[]{:S(2)}) copy-start(f32[64]{0:T(128)} %copy-done.200) | copy-start | bytes 772
  1405.7 244.4 %copy-start.104 = (bf16[1,1,64,1024]{3,2,1,0:T(8,128)(2,1)S(1)}, bf16[1,1,64,1024]{3,2,1,0:T(8,128)(2,1)}, u32[]{:S(2)}) copy-start(bf16[1,1,64,1024]{3,2,1,0:T(8,128)(2,1)} %get-tuple-element.78) | copy-start | bytes 393220
  1405.7 244.4 %copy-start.105 = (bf16[1,1,64,1024]{3,2,1,0:T(8,128)(2,1)S(1)}, bf16[1,1,64,1024]{3,2,1,0:T(8,128)(2,1)}, u32[]{:S(2)}) copy-start(bf16[1,1,64,1024]{3,2,1,0:T(8,128)(2,1)} %fusion.1094) | copy-start | bytes 393220
  1405.7 244.4 %copy-start.106 = (bf16[1,1,64,1024]{3,2,1,0:T(8,128)(2,1)S(1)}, bf16[1,1,64,1024]{3,2,1,0:T(8,128)(2,1)}, u32[]{:S(2)}) copy-start(bf16[1,1,64,1024]{3,2,1,0:T(8,128)(2,1)} %fusion.1095) | copy-start | bytes 393220
  1405.7 244.4 %copy-start.108 = (bf16[64,1024]{1,0:T(8,128)(2,1)S(1)}, bf16[64,1024]{1,0:T(8,128)(2,1)}, u32[]{:S(2)}) copy-start(bf16[64,1024]{1,0:T(8,128)(2,1)} %copy-done.107) | copy-start | bytes 393220
  (205 other events, 1451.8 us)
Sparse Core Ops, SparseCore 0:
  10.2 44.0 all-gather.32
  56.5 40.2 all-gather.36
  99.0 40.4 all-gather.30
  142.0 40.1 all-gather.34
  184.8 40.1 all-gather.38
  227.1 40.1 all-gather.40
  269.4 73.6 all-gather.42
  345.3 73.1 all-gather.44
  438.0 40.6 all-gather.46
  481.3 40.1 all-gather.48
  552.9 41.1 all-gather.54
  596.8 40.1 all-gather.56
  639.1 40.1 all-gather.62
  681.4 40.4 all-gather.64
  723.9 39.8 all-gather.58
  765.8 40.1 all-gather.60
  808.1 40.1 all-gather.50
  850.3 40.4 all-gather.52
  892.9 40.2 all-gather.70
  935.2 39.8 all-gather.72
  977.2 40.1 all-gather.66
  1019.6 40.6 all-gather.68
  1062.5 40.1 all-gather.74
  1116.2 37.2 all-gather.76
  1174.9 53.5 reduce-scatter.57
  1232.3 54.8 reduce-scatter.59
  1290.6 54.8 reduce-scatter.51
  1349.4 54.8 reduce-scatter.53
  1407.9 54.7 reduce-scatter.49
  1466.5 54.8 reduce-scatter.61
  1525.0 54.7 reduce-scatter.45
  1584.0 60.6 reduce-scatter.55
  1648.0 54.7 reduce-scatter.47
  1706.7 89.1 all-reduce.11
  1800.8 72.8 reduce-scatter.39
  1877.9 71.5 reduce-scatter.33
  1954.3 71.3 reduce-scatter.37
  2030.1 71.5 reduce-scatter.35
  2106.8 177.5 reduce-scatter.43
  2289.6 177.5 reduce-scatter.41
where the time goes:
time: 2490 us; the launch traced here: 2480 us
  waiting for transfers between devices  1580 us (63%)
  matrix products  421 us (17%)
  blocking collectives  193 us (8%)
  local copies, waits for them, and re-layouts  191 us (8%)
  other arithmetic  63.4 us (3%)
    unnamed x49, waiting for transfers between devices  331 us
    reduce_scatter x1, waiting for transfers between devices, sum_each(): lax.psum_scatter(grads[9][None], 'tok', scatter_dimension=1, tiled=True)  183 us
    reduce_scatter x1, waiting for transfers between devices, sum_each(): lax.psum_scatter(grads[11][None], 'tok', scatter_dimension=1, tiled=True)  183 us
    dot_general x18, matrix products, contract_rows(): jnp.einsum('tf,td->fd', left, right, preferred_element_type=jnp.float32)  120 us
    all_gather x6, waiting for transfers between devices, attention_forward(): lax.all_gather(value_rows, 'tok', axis=0, tiled=True)  120 us
    dot_general x33, matrix products, project(): return jnp.dot(left, right, preferred_element_type=jnp.float32)  110 us
    psum x1, waiting for transfers between devices, local(): prefix_sums = lax.psum((prefix_key_total, prefix_value_total), 'tok')  91.7 us
    all_gather x6, waiting for transfers between devices, attention_forward(): lax.all_gather(key_rows, 'tok', axis=0, tiled=True)  85.7 us
  transfers between devices with their start and end apart: 44, of which 30 were waited for; matrix products, arithmetic and copies ran while one was open for 25% of the time, Pallas kernels for 0%

commit v1 on v0

--- a/solution.py
+++ b/solution.py
@@ -1,6 +1,8 @@
 import jax
 import jax.numpy as jnp
 from jax import lax
+from jax.experimental import pallas as pl
+from jax.experimental.pallas import tpu as pltpu
 from jax.sharding import PartitionSpec as P
 
 HEADS = 16
@@ -558,6 +560,944 @@
     )
 
 
+MESH = pl.DeviceIdType.MESH
+F32 = jnp.float32
+BF16 = jnp.bfloat16
+ROWS = 64
+PIECE = 32
+BLOCK = 256
+SQRT_HALF = 0.7071067811865476
+INV_SQRT_2PI = 0.3989422804014327
+AG_X, AG_N, AG_Z, AG_O = range(4)
+RS_O, RS_Z, RS_N, RS_X = range(4)
+
+
+def flip(bit, other):
+    return bit + other - 2 * bit * other
+
+
+def mm(left, right):
+    return jnp.dot(left, right, preferred_element_type=F32)
+
+
+def mm_nt(left, right):
+    return lax.dot_general(left, right, (((1,), (1,)), ((), ())), preferred_element_type=F32)
+
+
+def mm_tn(left, right):
+    return lax.dot_general(left, right, (((0,), (0,)), ((), ())), preferred_element_type=F32)
+
+
+def rows_at(index, size):
+    return pl.ds(pl.multiple_of(index * size, size), size)
+
+
+def remote(src, dst, send, recv, device):
+    return pltpu.make_async_remote_copy(
+        src_ref=src, dst_ref=dst, send_sem=send, recv_sem=recv, device_id=device, device_id_type=MESH
+    )
+
+
+def local_copy(src, dst, sem):
+    return pltpu.make_async_copy(src, dst, sem)
+
+
+def bytes_of(ref, sem):
+    return pltpu.make_async_copy(ref, ref, sem)
+
+
+class Place:
+    def __init__(self):
+        self.x = lax.axis_index("section")
+        self.t = lax.axis_index("tok")
+        z = self.t // 4
+        self.y = (self.t // 2) % 2
+        self.core = self.t % 2
+        self.cube = z // 2
+        self.zl = z % 2
+        self.chip = self.x * 4 + self.zl * 2 + self.y
+        self.tau = self.chip * 2 + self.core
+
+    def device(self, x, cube):
+        return (x, cube * 8 + self.zl * 4 + self.y * 2 + self.core)
+
+    def twin(self):
+        return self.device(self.x, 1 - self.cube)
+
+    def sibling(self):
+        return (self.x, self.t + 1 - 2 * self.core)
+
+    def peer(self, r):
+        zl, y = flip(self.zl, (r // 2) % 2), flip(self.y, r % 2)
+        return (flip(self.x, r // 4), self.cube * 8 + zl * 4 + y * 2 + self.core)
+
+    def peer_chip(self, r):
+        return flip(self.x, r // 4) * 4 + flip(self.zl, (r // 2) % 2) * 2 + flip(self.y, r % 2)
+
+    def pair_rows(self, j):
+        return rows_at(flip(self.x, j // 2) * 2 + flip(self.zl, j % 2), BLOCK)
+
+
+class Gather:
+    HOPS = {(1, 0): (2, 3), (1, 1): (2, 3), (2, 0): (4, 6), (2, 1): (4, 6), (4, 0): (1, 5), (4, 1): (1, 5),
+            (3, 0): (4, 7), (6, 1): (1, 7)}
+
+    def __init__(self, place, buf, recv, sib, sends):
+        self.place, self.buf, self.recv, self.sib, self.sends = place, buf, recv, sib, sends
+
+    def piece(self, r, q, other=0):
+        core = flip(self.place.core, other)
+        row = (self.place.peer_chip(r) * 2 + core) * ROWS + q * PIECE
+        return self.buf.at[pl.ds(pl.multiple_of(row, PIECE), PIECE)]
+
+    def start(self):
+        for q in range(2):
+            own = self.piece(0, q)
+            for r in (4, 2, 1):
+                remote(own, own, self.sends.at[0, r, q], self.recv.at[r, q], self.place.peer(r)).start()
+            self.to_sibling(0, q).start()
+
+    def to_sibling(self, r, q):
+        rows = self.piece(r, q)
+        return remote(rows, rows, self.sends.at[1, r, q], self.sib.at[r, q], self.place.sibling())
+
+    def arrive(self, r, q):
+        rows = self.piece(r, q)
+        bytes_of(rows, self.recv.at[r, q]).wait()
+        if (r, q) in self.HOPS:
+            self.onward(r, q).start()
+        self.to_sibling(r, q).start()
+
+    def onward(self, r, q):
+        hop, seen = self.HOPS[(r, q)]
+        rows = self.piece(r, q)
+        return remote(rows, rows, self.sends.at[2, r, q], self.recv.at[seen, q], self.place.peer(hop))
+
+    def stage(self, number):
+        order = ((1, 2, 4), (3, 6, 5), (7,))[number]
+        for q in range(2):
+            for r in order:
+                self.arrive(r, q)
+
+    def ready(self, r):
+        for q in range(2):
+            bytes_of(self.piece(r, q, 1), self.sib.at[r, q]).wait()
+
+    def pair_ready(self, j):
+        self.ready(2 * j)
+        self.ready(2 * j + 1)
+
+    def blocks(self, use):
+        for j in range(4):
+            if j < 3:
+                self.stage(j)
+            self.pair_ready(j)
+            use(j)
+        self.drain()
+
+    def drain(self):
+        for q in range(2):
+            own = self.piece(0, q)
+            for r in (4, 2, 1):
+                bytes_of(own, self.sends.at[0, r, q]).wait()
+            for r in range(8):
+                bytes_of(own, self.sends.at[1, r, q]).wait()
+        for r, q in self.HOPS:
+            bytes_of(self.piece(0, q), self.sends.at[2, r, q]).wait()
+
+
+class Scatter:
+    def __init__(self, place, recv, sends, half, keep, sib_out, sib_in, out, inbox):
+        self.place, self.recv, self.sends = place, recv, sends
+        self.half, self.keep, self.sib_out, self.sib_in = half, keep, sib_out, sib_in
+        self.out, self.inbox = out, inbox
+
+    def pair(self, r):
+        return remote(
+            self.sib_out.at[r], self.sib_in.at[r], self.sends.at[0, r], self.recv.at[0, r], self.place.sibling()
+        )
+
+    def push(self, r):
+        return remote(
+            self.out.at[r], self.inbox.at[r], self.sends.at[1, r], self.recv.at[1, r], self.place.peer(r)
+        )
+
+    def give(self, j, partial):
+        for k in range(4):
+            self.half[k] = partial[k * ROWS : (k + 1) * ROWS]
+        core = self.place.core
+        for b in range(2):
+            r = 2 * j + flip(self.place.y, b)
+            self.keep[r] = self.half[2 * b + core]
+            self.sib_out[r] = self.half[2 * b + 1 - core].astype(BF16)
+            self.pair(r).start()
+
+    def forward(self, j):
+        for k in (1, 0):
+            r = 2 * j + k
+            self.pair(r).wait_recv()
+            total = self.keep[r] + self.sib_in[r].astype(F32)
+
+            @pl.when(r == 0)
+            def _():
+                self.keep[0] = total
+
+            @pl.when(r != 0)
+            def _():
+                self.out[r] = total.astype(BF16)
+                self.push(r).start()
+
+    def run(self, produce):
+        def step(i, carry):
+            @pl.when(i < 4)
+            def _():
+                self.give(3 - i, produce(3 - i))
+
+            @pl.when(i >= 1)
+            def _():
+                self.forward(4 - i)
+
+            return carry
+
+        lax.fori_loop(0, 5, step, 0)
+
+    def finish(self):
+        def collect(r, carry):
+            self.push(r).wait_recv()
+            self.keep[0] = self.keep[0] + self.inbox[r].astype(F32)
+            return carry
+
+        lax.fori_loop(1, 8, collect, 0)
+
+        def drain(r, carry):
+            self.pair(r).wait_send()
+
+            @pl.when(r >= 1)
+            def _():
+                self.push(r).wait_send()
+
+            return carry
+
+        lax.fori_loop(0, 8, drain, 0)
+        return self.keep[0]
+
+
+def norm_forward(value, gain, shift, hat_ref, rstd_ref):
+    centred = value - jnp.mean(value, axis=-1, keepdims=True)
+    rstd = lax.rsqrt(jnp.mean(centred * centred, axis=-1, keepdims=True) + 1e-05)
+    hat = centred * rstd
+    hat_ref[...] = hat
+    rstd_ref[...] = jnp.broadcast_to(rstd, rstd_ref.shape)
+    return hat * gain + shift
+
+
+def norm_backward(upstream, gain, hat_ref, rstd_ref):
+    hat = hat_ref[...]
+    scaled = upstream * gain
+    mean_one = jnp.mean(scaled, axis=-1, keepdims=True)
+    mean_two = jnp.mean(scaled * hat, axis=-1, keepdims=True)
+    result = rstd_ref[:, :1] * (scaled - mean_one - hat * mean_two)
+    d_gain = jnp.sum(upstream * hat, axis=0, keepdims=True)
+    d_shift = jnp.sum(upstream, axis=0, keepdims=True)
+    return result, d_gain, d_shift
+
+
+def column_sum(low):
+    return jnp.sum(low.astype(F32), axis=0, keepdims=True)
+
+
+def kernel(
+    lengths, inputs, cotangent, wqkv_src, wup_src, wdn_src, wout_src, pk_src, pv_src,
+    out_y, out_dx, got_qkv, got_up, got_dn, got_out, got_prefix, got_rows, got_bias,
+    ag_recv, ag_sib, ag_send, rs_recv, rs_send,
+    wsend, wown, wtwin, wrelay, psem, xsem, osend, orecv, tsend, trecv, gsend, grecv,
+    wqkv, wup, wdn, wout, pre,
+    qseg, kseg, xg, ng, dzg, dog, param,
+    qs, ks, vs, kt, vt, lse, ctb, ctf,
+    hat1, rstd1, hat2, rstd2, act, dact,
+    half, keep, sib_out, sib_in, rs_out, inbox,
+    own_a, own_b, ystage, dstage,
+    dfs, dcb, delta, dqt, dkacc, dvacc, dqkv, dqkvt,
+    rowacc, biasacc, g_qkv, g_up, g_dn, g_out, g_prefix,
+    t_qkv, t_up, t_dn, t_out, t_prefix,
+):
+    place = Place()
+    x, t, cube, core, tau = place.x, place.t, place.cube, place.core, place.tau
+    tokens = qs.shape[1]
+    width = xg.shape[2]
+    half_rows = 8 * ROWS
+    barrier = pltpu.get_barrier_semaphore()
+
+    def greet(i, carry):
+        gx, gt = i // 16, i % 16
+
+        @pl.when((gx != x) | (gt != t))
+        def _():
+            pl.semaphore_signal(barrier, inc=1, device_id=(gx, gt), device_id_type=MESH)
+
+        return carry
+
+    lax.fori_loop(0, 32, greet, 0)
+    pl.semaphore_wait(barrier, 31)
+
+    own_rows = rows_at(tau, ROWS)
+    x_here = local_copy(inputs.at[cube], xg.at[0, own_rows], xsem.at[0])
+    x_there = remote(inputs.at[1 - cube], xg.at[0, own_rows], xsem.at[1], xsem.at[2], place.twin())
+    d_here = local_copy(cotangent.at[cube], dstage.at[2], xsem.at[3])
+    d_there = remote(cotangent.at[1 - cube], dstage.at[2], xsem.at[4], xsem.at[5], place.twin())
+
+    @pl.when(x == cube)
+    def _():
+        x_there.start()
+        x_here.start()
+
+    def spread_out(kind):
+        src_all, dst_all = ((wqkv_src, wqkv), (wup_src, wup))[kind]
+
+        def one(k, carry):
+            to = lax.rem(k + tau + 1, 16)
+            src, dst = src_all.at[to], dst_all.at[rows_at(x * 16 + t, ROWS)]
+            sem = wown.at[kind, x, t % 8]
+
+            @pl.when(to == tau)
+            def _():
+                local_copy(src, dst, sem).start()
+
+            @pl.when(to != tau)
+            def _():
+                remote(src, dst, wsend.at[kind], sem, (to // 8, cube * 8 + to % 8)).start()
+
+            return carry
+
+        lax.fori_loop(0, 16, one, 0)
+
+    def slices_out():
+        for side in range(2):
+            src = wdn_src.at[0, pl.ds(side * 128, 128)]
+            dst = wdn.at[x, rows_at(cube, 128)]
+            pl.when(x == side)(local_copy(src, dst, wown.at[3, x, 0]).start)
+            pl.when(x != side)(remote(src, dst, wsend.at[3], wown.at[3, x, 0], place.device(1 - x, cube)).start)
+        src, dst = wout_src.at[0], wout.at[x]
+        pl.when(x == cube)(local_copy(src, dst, wown.at[2, x, 0]).start)
+        pl.when(x != cube)(remote(src, dst, wsend.at[2], wown.at[2, x, 0], place.device(1 - x, cube)).start)
+
+    def prefix_out():
+        for side, index in ((x, 0), (1 - x, 1)):
+            for kind, src_all in ((0, pk_src), (1, pv_src)):
+                src = src_all.at[0, :, rows_at(side * 4 + place.zl * 2 + place.y, 128)]
+                dst = pre.at[x, kind]
+                if index == 0:
+                    yield local_copy(src, dst, psem.at[0, kind])
+                else:
+                    yield remote(src, dst, psem.at[1, kind], psem.at[2, kind], place.device(1 - x, cube))
+
+    def twin_copy(kind, l):
+        if kind < 2:
+            ref = (wqkv, wup)[kind].at[rows_at(l * 2 + cube, half_rows)]
+        elif kind == 3:
+            ref = wdn.at[l, rows_at(cube, 128)]
+        else:
+            ref = wout.at[l]
+        return remote(ref, ref, wrelay.at[kind, l], wtwin.at[kind, l], place.twin())
+
+    def relay_blocks(kind, l):
+        ref_all = (wqkv, wup)[kind]
+
+        def one(k, carry):
+            ref = ref_all.at[rows_at((l * 2 + cube) * 8 + k, ROWS)]
+            bytes_of(ref, wown.at[kind, l, k]).wait()
+            remote(ref, ref, wrelay.at[kind, l], wtwin.at[kind, l], place.twin()).start()
+            return carry
+
+        lax.fori_loop(0, 8, one, 0)
+
+    def relay_slices(l):
+        dn = wdn.at[l, rows_at(cube, 128)]
+        bytes_of(dn, wown.at[3, l, 0]).wait()
+        twin_copy(3, l).start()
+
+        @pl.when(x == cube)
+        def _():
+            bytes_of(wout.at[l], wown.at[2, l, 0]).wait()
+            twin_copy(2, l).start()
+
+    def weights_in(kind, l):
+        if kind < 2:
+            ref = (wqkv, wup)[kind].at[rows_at(l * 2 + 1 - cube, half_rows)]
+        elif kind == 3:
+            ref = wdn.at[l, rows_at(1 - cube, 128)]
+        else:
+            ref = wout.at[l]
+        wait = bytes_of(ref, wtwin.at[kind, l]).wait
+        if kind == 2:
+            pl.when(x != cube)(wait)
+        else:
+            wait()
+
+    def weights_drain():
+        for kind, ref in ((0, wqkv), (1, wup)):
+            bytes_of(ref.at[pl.ds(0, 15 * ROWS)], wsend.at[kind]).wait()
+        bytes_of(wdn.at[0, pl.ds(0, 128)], wsend.at[3]).wait()
+        pl.when(x != cube)(bytes_of(wout.at[0], wsend.at[2]).wait)
+        for l in range(2):
+            for kind in (0, 1, 3):
+                twin_copy(kind, l).wait_send()
+            pl.when(x == cube)(twin_copy(2, l).wait_send)
+
+    def weight(ref, l):
+        return ref[rows_at(l, 16 * ROWS)]
+
+    def own_half(pair):
+        return jnp.where(core == 0, pair[:, :64], pair[:, 64:])
+
+    def gather(buf, phase):
+        return Gather(place, buf, ag_recv.at[phase], ag_sib.at[phase], ag_send)
+
+    def scatter(phase):
+        boxes = phase % 2
+        return Scatter(
+            place, rs_recv.at[phase], rs_send, half, keep, sib_out, sib_in.at[boxes], rs_out, inbox.at[boxes]
+        )
+
+    prefixes = list(prefix_out())
+    for copy in prefixes:
+        copy.start()
+
+    @pl.when(x == 0)
+    def _():
+        spread_out(0)
+
+    rowacc[...] = jnp.zeros_like(rowacc)
+    biasacc[...] = jnp.zeros_like(biasacc)
+    dqt[64:128] = jnp.zeros((64, tokens), F32)
+    along = lax.broadcasted_iota(jnp.int32, (8, tokens), 1)
+    down = lax.broadcasted_iota(jnp.int32, (tokens, 128), 0)
+    segment_q, segment_k = jnp.zeros((8, tokens), jnp.int32), jnp.zeros((tokens, 128), jnp.int32)
+    end = jnp.int32(0)
+    for j in range(lengths.shape[1]):
+        end = end + lengths[cube, j]
+        segment_q = segment_q + (along >= end).astype(jnp.int32)
+        segment_k = segment_k + (down >= end).astype(jnp.int32)
+    qseg[...] = segment_q
+    kseg[0:tokens] = segment_k
+    kseg[tokens:] = jnp.full((kseg.shape[0] - tokens, 128), -1, jnp.int32)
+
+    pl.when(x != cube)(x_there.wait_recv)
+    pl.when(x == cube)(x_here.wait)
+
+    def result_out(stage, out, kind, layer):
+        dst = out.at[cube]
+        is_self = (layer == x) & (x == cube)
+        here = local_copy(stage, dst, orecv.at[kind, cube])
+        there = remote(stage, dst, osend.at[kind, layer], orecv.at[kind, cube], place.device(layer, x))
+        return is_self, here, there
+
+    def visible(cols):
+        key_part = kseg[...]
+        keys_two = jnp.concatenate([key_part, key_part], axis=1)
+        return (keys_two == qseg[0:1, cols]) | (keys_two < 0)
+
+    def forward_layer(l, carry):
+        gather_x = gather(xg.at[l], AG_X)
+        gather_x.start()
+
+        @pl.when(l == 0)
+        def _():
+            @pl.when(x == 0)
+            def _():
+                spread_out(1)
+                slices_out()
+
+            @pl.when(x == cube)
+            def _():
+                d_there.start()
+                d_here.start()
+
+            for number in range(3):
+                gather_x.stage(number)
+            relay_blocks(0, 0)
+            for copy in prefixes[:2]:
+                copy.wait()
+            for copy in prefixes[2:]:
+                copy.wait()
+
+        weights_in(0, l)
+        tail = wqkv[rows_at(l, 16 * ROWS), 128:256].astype(F32).T
+        param[l] = tail[64:80]
+        biases = own_half(param[l, 0:8, rows_at(tau // 2, 128)])[6:8]
+        empty = jnp.zeros((1, 64), F32)
+        qkv_bias = jnp.concatenate([biases[0:1], empty, biases[1:2], empty], axis=1)
+        prefix = jnp.concatenate(
+            [own_half(pre[l, 0].astype(F32)), own_half(pre[l, 1].astype(F32))], axis=1
+        )
+        ks[l, tokens:] = prefix[:, :64].astype(BF16)
+        vs[l, tokens:] = prefix[:, 64:].astype(BF16)
+        prefix_t = prefix.T
+        kt[l, :, tokens:] = prefix_t[:64].astype(BF16)
+        vt[l, :, tokens:] = prefix_t[64:].astype(BF16)
+
+        for j in range(4):
+            if j < 3:
+                @pl.when(l == 1)
+                def _():
+                    gather_x.stage(j)
+
+            gather_x.pair_ready(j)
+            rows = place.pair_rows(j)
+            value = mm(xg[l, rows], weight(wqkv, l)) + qkv_bias
+            qs[l, rows] = (value[:, :64] * 0.125).astype(BF16)
+            ks[l, rows] = value[:, 64:128].astype(BF16)
+            vs[l, rows] = value[:, 128:192].astype(BF16)
+            value_t = value.T
+            kt[l, :, rows] = value_t[64:128].astype(BF16)
+            vt[l, :, rows] = value_t[128:192].astype(BF16)
+        gather_x.drain()
+
+        @pl.when(l == 0)
+        def _():
+            relay_slices(0)
+            relay_blocks(1, 0)
+
+            @pl.when(x == 1)
+            def _():
+                spread_out(0)
+                slices_out()
+                spread_out(1)
+
+        scatter_o = scatter(RS_O)
+
+        def attend(j):
+            cols = place.pair_rows(j)
+            scores = jnp.where(visible(cols), mm_nt(ks[l], qs[l, cols]), NEGATIVE)
+            top = jnp.max(scores, axis=0, keepdims=True)
+            grown = jnp.exp(scores - top)
+            total = jnp.sum(grown, axis=0, keepdims=True)
+            probs = (grown * (1.0 / total)).astype(BF16)
+            lse[l, 0:1, cols] = top + jnp.log(total)
+            context_t = mm(vt[l], probs)
+            ctf[l, :, cols] = context_t
+            low = context_t.astype(BF16)
+            ctb[l, :, cols] = low
+            return mm_tn(low, wout[l])
+
+        pl.when(l == 0)(lambda: weights_in(2, 0))
+        pl.when(l == 1)(lambda: weights_in(2, 1))
+        scatter_o.run(attend)
+        attended = scatter_o.finish() + param[l, 0:1]
+        normal = norm_forward(
+            xg[l, own_rows].astype(F32) + attended,
+            param[l, 1:2], param[l, 2:3], hat1.at[l], rstd1.at[l],
+        )
+        own_a[...] = normal
+        ng[l, own_rows] = normal.astype(BF16)
+        gather_n = gather(ng.at[l], AG_N)
+        gather_n.start()
+
+        @pl.when(l == 0)
+        def _():
+            relay_blocks(0, 1)
+
+        weights_in(1, l)
+        weights_in(3, l)
+        up_part = own_half(param[l, 8:16, rows_at(place.zl * 2 + place.y, 128)])
+        up_more = own_half(param[l, 8:16, rows_at(4 + place.zl * 2 + place.y, 128)])
+        up_parts = jnp.where(x == 0, up_part[0:2], up_part[2:4])
+        up_more = jnp.where(x == 0, up_more[0:2], up_more[2:4])
+        up_bias = jnp.concatenate([up_parts[0:1], up_parts[1:2], up_more[0:1], up_more[1:2]], axis=1)
+        scatter_z = scatter(RS_Z)
+
+        def feed_block(j):
+            rows = place.pair_rows(j)
+            value = mm(ng[l, rows], weight(wup, l)) + up_bias
+            cdf = 0.5 * (1.0 + lax.erf(value * SQRT_HALF))
+            low = (value * cdf).astype(BF16)
+            act[l, rows] = low
+            dact[l, rows] = cdf + value * (jnp.exp(-0.5 * value * value) * INV_SQRT_2PI)
+            scatter_z.give(j, mm(low, wdn[l]))
+            if j:
+                scatter_z.forward(j - 1)
+
+        gather_n.blocks(feed_block)
+        scatter_z.forward(3)
+
+        @pl.when(l == 0)
+        def _():
+            relay_slices(1)
+            relay_blocks(1, 1)
+
+        mixed = scatter_z.finish() + param[l, 3:4]
+        result = norm_forward(
+            own_a[...] + mixed, param[l, 4:5], param[l, 5:6], hat2.at[l], rstd2.at[l]
+        ).astype(BF16)
+        ystage[l] = result
+
+        @pl.when(l == 0)
+        def _():
+            xg[1, own_rows] = result
+
+        is_self, here, there = result_out(ystage.at[l], out_y, 0, l)
+        pl.when(is_self)(here.start)
+        pl.when(jnp.logical_not(is_self))(there.start)
+        return carry
+
+    lax.fori_loop(0, 2, forward_layer, 0)
+
+    pl.when(x != cube)(d_there.wait_recv)
+    pl.when(x == cube)(d_here.wait)
+
+    other_half, this_half = 1 - cube, cube
+
+    def twin_parts(kind, l):
+        if kind < 2:
+            ref, box = ((g_qkv, t_qkv), (g_up, t_up))[kind]
+            return ref.at[l, rows_at(other_half, half_rows)], box, ref.at[l, rows_at(this_half, half_rows)]
+        if kind == 2:
+            return g_prefix.at[l, rows_at(other_half, 32)], t_prefix, g_prefix.at[l, rows_at(this_half, 32)]
+        if kind == 3:
+            return g_dn.at[l, rows_at(other_half, 128)], t_dn, g_dn.at[l, rows_at(this_half, 128)]
+        return g_out.at[l], t_out, g_out.at[l]
+
+    def twin_send(kind, l):
+        src, box, own = twin_parts(kind, l)
+        return remote(src, box.at[l], tsend.at[kind, l], trecv.at[kind, l], place.twin())
+
+    def twin_start(kind, l):
+        copy = twin_send(kind, l)
+        if kind == 4:
+            pl.when(x != cube)(copy.start)
+        else:
+            copy.start()
+
+    def owner_copies(kind, l, act_on):
+        src, box, own = twin_parts(kind, l)
+        mine = x == l
+        if kind < 2:
+            got = (got_qkv, got_up)[kind]
+
+            def one(k, carry):
+                to = lax.rem(k + t + 1, 8)
+                src, dst = own.at[rows_at(to, ROWS)], got.at[tau]
+                is_self = mine & (to == t % 8)
+                act_on(is_self, src, dst, (l, cube * 8 + to))
+                return carry
+
+            lax.fori_loop(0, 8, one, 0)
+        elif kind == 2:
+
+            def one(k, carry):
+                to = lax.rem(k + t + 1, 16)
+                act_on(mine & (to == t), own, got_prefix.at[tau, rows_at(this_half, 32)], (l, to))
+                return carry
+
+            lax.fori_loop(0, 16, one, 0)
+        elif kind == 3:
+            act_on(mine, own, got_dn.at[rows_at(x, 128)], place.device(l, cube))
+        else:
+
+            @pl.when(x == cube)
+            def _():
+                act_on(mine, own, got_out, place.device(l, cube))
+
+    def start_on(kind, l):
+        def act_on(is_self, src, dst, dev):
+            pl.when(is_self)(local_copy(src, dst, grecv.at[kind]).start)
+            pl.when(jnp.logical_not(is_self))(remote(src, dst, gsend.at[kind, l], grecv.at[kind], dev).start)
+
+        return act_on
+
+    def owner_start(kind, l):
+        src, box, own = twin_parts(kind, l)
+
+        def add():
+            twin_send(kind, l).wait_recv()
+            own[...] = (own[...].astype(F32) + box[l].astype(F32)).astype(BF16)
+
+        if kind == 4:
+            pl.when(x == cube)(add)
+        else:
+            add()
+        owner_copies(kind, l, start_on(kind, l))
+
+    def grads_drain(l):
+        for kind in range(5):
+            if kind == 4:
+                pl.when(x != cube)(twin_send(kind, l).wait_send)
+            else:
+                twin_send(kind, l).wait_send()
+        for kind, ref in ((0, got_qkv), (1, got_up)):
+            pl.when(x == l)(bytes_of(ref.at[pl.ds(0, 7)], gsend.at[kind, l]).wait)
+            pl.when(x != l)(bytes_of(ref.at[pl.ds(0, 8)], gsend.at[kind, l]).wait)
+        for count, condition in ((15, x == l), (16, x != l)):
+            pl.when(condition)(bytes_of(got_prefix.at[pl.ds(0, count), pl.ds(0, 32)], gsend.at[2, l]).wait)
+            pl.when(condition)(bytes_of(got_rows.at[pl.ds(0, count)], gsend.at[5, l]).wait)
+        pl.when(x != l)(bytes_of(g_dn.at[0, pl.ds(0, 128)], gsend.at[3, l]).wait)
+        pl.when((x != l) & (x == cube))(bytes_of(g_out.at[0], gsend.at[4, l]).wait)
+        for to, src, dst in bias_pairs(l):
+            is_self = (x == l) & (cube == to)
+            pl.when(jnp.logical_not(is_self))(bytes_of(src, gsend.at[6 + to, l]).wait)
+
+    def rows_start(l):
+        def one(k, carry):
+            to = lax.rem(k + t + 1, 16)
+            src, dst = rowacc.at[l, :, rows_at(to // 2, 128)], got_rows.at[cube * 16 + tau]
+            is_self = (x == l) & (to == t)
+            pl.when(is_self)(local_copy(src, dst, grecv.at[5]).start)
+            pl.when(jnp.logical_not(is_self))(remote(src, dst, gsend.at[5, l], grecv.at[5], (l, to)).start)
+            return carry
+
+        lax.fori_loop(0, 16, one, 0)
+
+    def bias_pairs(l):
+        for to in range(2):
+            yield to, biasacc.at[l], got_bias.at[cube * 2 + x]
+
+    def bias_start(l):
+        for to, src, dst in bias_pairs(l):
+            is_self = (x == l) & (cube == to)
+            pl.when(is_self)(local_copy(src, dst, grecv.at[6]).start)
+            pl.when(jnp.logical_not(is_self))(
+                remote(src, dst, gsend.at[6 + to, l], grecv.at[6], place.device(l, to)).start
+            )
+
+    def backward_layer(step, carry):
+        l = 1 - step
+        upstream = dstage[l + 1].astype(F32)
+        d_sum, d_gain, d_shift = norm_backward(upstream, param[l, 4:5], hat2.at[l], rstd2.at[l])
+        own_b[...] = d_sum
+        low = d_sum.astype(BF16)
+        dzg[own_rows] = low
+        gather_z = gather(dzg, AG_Z)
+        gather_z.start()
+        rowacc[l, 3:4] = d_gain
+        rowacc[l, 4:5] = d_shift
+        rowacc[l, 5:6] = column_sum(low)
+        scatter_n = scatter(RS_N)
+
+        def back_block(j):
+            rows = place.pair_rows(j)
+            low = (dact[l, rows] * mm_nt(dzg[rows], wdn[l])).astype(BF16)
+            dfs[rows] = low
+            scatter_n.give(j, mm_nt(low, weight(wup, l)))
+            if j:
+                scatter_n.forward(j - 1)
+
+        gather_z.blocks(back_block)
+        scatter_n.forward(3)
+        biasacc[l, 1:2] = column_sum(dfs[...])
+
+        def down_tile(i, carry):
+            cols = rows_at(i, 256)
+            g_dn[l, :, cols] = mm_tn(act[l], dzg[:, cols]).astype(BF16)
+            return carry
+
+        lax.fori_loop(0, width // 256, down_tile, 0)
+
+        def up_tile(i, carry):
+            cols = rows_at(i, 256)
+            g_up[l, cols] = mm_tn(ng[l, :, cols], dfs[...]).astype(BF16)
+            return carry
+
+        lax.fori_loop(0, width // 256, up_tile, 0)
+        twin_start(3, l)
+        twin_start(1, l)
+
+        @pl.when(step == 1)
+        def _():
+            owner_start(0, 1)
+            owner_start(4, 1)
+
+        d_normal = own_b[...] + scatter_n.finish()
+        d_sum, d_gain, d_shift = norm_backward(d_normal, param[l, 1:2], hat1.at[l], rstd1.at[l])
+        own_a[...] = d_sum
+        low = d_sum.astype(BF16)
+        dog[own_rows] = low
+        gather_o = gather(dog, AG_O)
+        gather_o.start()
+        rowacc[l, 0:1] = d_gain
+        rowacc[l, 1:2] = d_shift
+        rowacc[l, 2:3] = column_sum(low)
+        rows_start(l)
+        dkacc[...] = jnp.zeros_like(dkacc)
+        dvacc[...] = jnp.zeros_like(dvacc)
+
+        def attend_back(j):
+            cols = place.pair_rows(j)
+            d_context = mm_nt(dog[cols], wout[l]).astype(BF16)
+            dcb[cols] = d_context
+            d_context_t = mm_nt(wout[l], dog[cols]).astype(BF16).astype(F32)
+            sums = jnp.sum(d_context_t * ctf[l, :, cols], axis=0, keepdims=True)
+            scores = jnp.where(visible(cols), mm_nt(ks[l], qs[l, cols]), NEGATIVE)
+            probs = jnp.exp(scores - lse[l, 0:1, cols])
+            d_probs = mm_nt(vs[l], d_context)
+            d_scores = (probs * (d_probs - sums)).astype(BF16)
+            dvacc[...] += mm(probs.astype(BF16), d_context)
+            dkacc[...] += mm(d_scores, qs[l, cols])
+            dqt[0:64, cols] = mm(kt[l], d_scores) * 0.125
+
+        gather_o.blocks(attend_back)
+        g_prefix[l] = jnp.concatenate([dkacc[tokens:], dvacc[tokens:]], axis=1).astype(BF16)
+        twin_start(2, l)
+        scatter_x = scatter(RS_X)
+
+        def assemble(j):
+            rows = place.pair_rows(j)
+            d_query = dqt[:, rows].T[:, :64]
+            value = jnp.concatenate(
+                [d_query, dkacc[rows], dvacc[rows], jnp.zeros((BLOCK, 64), F32)], axis=1
+            )
+            low = value.astype(BF16)
+            dqkv[rows] = low
+            dqkvt[:, rows] = value.T.astype(BF16)
+            return mm_nt(low, weight(wqkv, l))
+
+        scatter_x.run(assemble)
+        biasacc[l, 0:1] = column_sum(dqkv[...])
+        bias_start(l)
+
+        def qkv_tile(i, carry):
+            cols = rows_at(i, 256)
+            g_qkv[l, cols] = mm(dqkvt[...], xg[l, :, cols]).T.astype(BF16)
+            return carry
+
+        lax.fori_loop(0, width // 256, qkv_tile, 0)
+        twin_start(0, l)
+        g_out[l] = mm(ctb[l], dog[...]).astype(BF16)
+        twin_start(4, l)
+        for kind in (3, 1, 2):
+            owner_start(kind, l)
+
+        dstage[l] = (own_a[...] + scatter_x.finish()).astype(BF16)
+        is_self, here, there = result_out(dstage.at[l], out_dx, 1, l)
+        pl.when(is_self)(here.start)
+        pl.when(jnp.logical_not(is_self))(there.start)
+        return carry
+
+    lax.fori_loop(0, 2, backward_layer, 0)
+    owner_start(0, 0)
+    owner_start(4, 0)
+
+    @pl.when(x == cube)
+    def _():
+        x_there.wait_send()
+        d_there.wait_send()
+
+    weights_drain()
+    for l in range(2):
+        grads_drain(l)
+        for kind, stage, out in ((0, ystage.at[l], out_y), (1, dstage.at[l], out_dx)):
+            is_self, here, there = result_out(stage, out, kind, l)
+            pl.when(jnp.logical_not(is_self))(there.wait_send)
+    for kind, out in ((0, out_y), (1, out_dx)):
+        for m in range(2):
+            bytes_of(out.at[m], orecv.at[kind, m]).wait()
+    for kind, ref in enumerate((got_qkv, got_up, got_prefix, got_dn, got_out, got_rows, got_bias)):
+        bytes_of(ref, grecv.at[kind]).wait()
+
+
+def cube_local(
+    inputs, cotangent, lengths, prefix_keys, prefix_values,
+    w_query, b_query, w_key, w_value, b_value, w_out, b_out, norm1_gain, norm1_shift,
+    w_up, b_up, w_down, b_down, norm2_gain, norm2_shift,
+):
+    t = lax.axis_index("tok")
+    rows, width = w_query.shape[1], w_query.shape[2]
+    heads = width // HEAD
+    tokens = inputs.shape[1] * lax.axis_size("tok")
+    prefix = prefix_keys.shape[1]
+    keys = tokens + prefix
+    hidden = b_up.shape[1]
+
+    def by_head(value):
+        return value[0].reshape(rows, heads, HEAD).transpose(1, 0, 2)
+
+    vectors = jnp.concatenate(
+        [b_out, norm1_gain, norm1_shift, b_down, norm2_gain, norm2_shift, b_query, b_value,
+         b_up.reshape(4, HEAD), jnp.zeros((HEAD - 12, HEAD), BF16)], axis=0,
+    ).T
+    wqkv_src = jnp.concatenate(
+        [by_head(w_query), by_head(w_key), by_head(w_value),
+         jnp.broadcast_to(vectors[None], (heads, rows, HEAD))], axis=-1,
+    )
+    wup_src = w_up[0].reshape(rows, 2, 8, 2, 128).transpose(3, 2, 0, 1, 4).reshape(heads, rows, 256)
+    anywhere = pl.BlockSpec(memory_space=pl.ANY)
+    smem = pl.BlockSpec(memory_space=pltpu.SMEM)
+    dma = pltpu.SemaphoreType.DMA
+    V = pltpu.VMEM
+    L = 2
+    shape = jax.ShapeDtypeStruct
+    results = pl.pallas_call(
+        kernel,
+        out_shape=(
+            shape((2, ROWS, width), BF16), shape((2, ROWS, width), BF16),
+            shape((16, ROWS, 256), BF16), shape((16, ROWS, 256), BF16),
+            shape((hidden, width), BF16), shape((ROWS, width), BF16),
+            shape((16, prefix, 128), BF16), shape((32, 8, 128), F32), shape((4, 8, 256), F32),
+        ),
+        in_specs=[smem] + [anywhere] * 8,
+        out_specs=[anywhere] * 9,
+        scratch_shapes=[
+            dma((4, 8, 2)), dma((4, 8, 2)), dma((3, 8, 2)), dma((4, 2, 8)), dma((2, 8)),
+            dma((4,)), dma((4, 2, 8)), dma((4, 2)), dma((4, 2)), dma((3, 2)), dma((6,)),
+            dma((2, 2)), dma((2, 2)), dma((5, 2)), dma((5, 2)), dma((8, 2)), dma((7,)),
+            V((L * 1024, 256), BF16), V((L * 1024, 256), BF16), V((L, hidden, width), BF16),
+            V((L, ROWS, width), BF16), V((L, 2, prefix, 128), BF16),
+            V((8, tokens), jnp.int32), V((keys, 128), jnp.int32),
+            V((L, tokens, width), BF16), V((L, tokens, width), BF16),
+            V((tokens, width), BF16), V((tokens, width), BF16), V((L, 16, width), F32),
+            V((L, tokens, HEAD), BF16), V((L, keys, HEAD), BF16), V((L, keys, HEAD), BF16),
+            V((L, HEAD, keys), BF16), V((L, HEAD, keys), BF16),
+            V((L, 8, tokens), F32), V((L, HEAD, tokens), BF16), V((L, HEAD, tokens), F32),
+            V((L, ROWS, width), F32), V((L, ROWS, 128), F32), V((L, ROWS, width), F32), V((L, ROWS, 128), F32),
+            V((L, tokens, hidden), BF16), V((L, tokens, hidden), F32),
+            V((4, ROWS, width), F32), V((8, ROWS, width), F32), V((8, ROWS, width), BF16),
+            V((2, 8, ROWS, width), BF16), V((8, ROWS, width), BF16), V((2, 8, ROWS, width), BF16),
+            V((ROWS, width), F32), V((ROWS, width), F32), V((L, ROWS, width), BF16), V((L + 1, ROWS, width), BF16),
+            V((tokens, hidden), BF16), V((tokens, HEAD), BF16), V((8, tokens), F32), V((128, tokens), F32),
+            V((keys, HEAD), F32), V((keys, HEAD), F32), V((tokens, 256), BF16), V((256, tokens), BF16),
+            V((L, 8, width), F32), V((L, 8, 256), F32),
+            V((L, width, 256), BF16), V((L, width, 256), BF16), V((L, hidden, width), BF16),
+            V((L, ROWS, width), BF16), V((L, prefix, 128), BF16),
+            V((L, width // 2, 256), BF16), V((L, width // 2, 256), BF16), V((L, hidden // 2, width), BF16),
+            V((L, ROWS, width), BF16), V((L, prefix // 2, 128), BF16),
+        ],
+        compiler_params=pltpu.CompilerParams(
+            collective_id=0, has_side_effects=True, vmem_limit_bytes=60 * 2**20
+        ),
+    )(lengths, inputs, cotangent, wqkv_src, wup_src, w_down, w_out, prefix_keys, prefix_values)
+    out_y, out_dx, got_qkv, got_up, got_dn, got_out, got_prefix, got_rows, got_bias = results
+
+    def side_by_side(value):
+        return value.astype(F32).transpose(1, 0, 2).reshape(1, value.shape[1], -1)
+
+    up = got_up.reshape(2, 8, rows, 2, 128).transpose(2, 3, 1, 0, 4).astype(F32)
+    row_sum = lax.dynamic_slice_in_dim(jnp.sum(got_rows, axis=0), (t % 2) * 64, 64, 1)
+    side = t // 8
+    bias = got_bias[:2] + got_bias[2:]
+    bias_up = lax.dynamic_slice_in_dim(bias[:, 1], side * 128, 128, 1).reshape(1, hidden)
+    bias_qkv = lax.dynamic_index_in_dim(bias[:, 0], side, 0, keepdims=True)
+    return (
+        out_y[None],
+        out_dx[None],
+        side_by_side(got_qkv[:, :, :64]),
+        bias_qkv[:, 0:64],
+        side_by_side(got_qkv[:, :, 64:128]),
+        side_by_side(got_qkv[:, :, 128:192]),
+        bias_qkv[:, 128:192],
+        got_out[None].astype(F32),
+        row_sum[2:3],
+        row_sum[0:1],
+        row_sum[1:2],
+        up.reshape(1, rows, -1),
+        bias_up,
+        got_dn[None].astype(F32),
+        row_sum[5:6],
+        row_sum[3:4],
+        row_sum[4:5],
+        side_by_side(got_prefix[:, :, :64]),
+        side_by_side(got_prefix[:, :, 64:]),
+    )
+
+
 def solution(mesh):
     placed = (
         P(None, "tok", None),
@@ -582,7 +1522,7 @@
         P("section", "tok"),
     )
     return jax.shard_map(
-        local,
+        cube_local if mesh.shape["tok"] == HEADS else local,
         mesh=mesh,
         in_specs=placed,
         out_specs=(

time: 2490 us -> 408 us (0.16)
  waiting for transfers between devices: 1580 us -> 0 us
  matrix products: 421 us -> 0 us
  Pallas kernels: 0 us -> 374 us
  blocking collectives: 193 us -> 0 us
  local copies, waits for them, and re-layouts: 191 us -> 24 us
  other arithmetic: 63.4 us -> 5.36 us
    reduce_scatter x6 -> x0, waiting for transfers between devices: 671 us -> none  [the longest x1 183 us: sum_each(): lax.psum_scatter(grads[9][None], 'tok', scatter_dimension=1, tiled=True)]
    all_gather x24 -> x0, waiting for transfers between devices: 465 us -> none  [the longest x6 120 us: attention_forward(): lax.all_gather(value_rows, 'tok', axis=0, tiled=True)]
    dot_general x117 -> x0, matrix products: 421 us -> none  [the longest x18 120 us: contract_rows(): jnp.einsum('tf,td->fd', left, right, preferred_element_type=jnp.float32)]
    pallas_call x0 -> x1, Pallas kernels: none -> 374 us  [cube_local(): pl.pallas_call(kernel, out_shape=(shape((2, ROWS, width), BF16), shape((2...]
    unnamed x49 -> x0, waiting for transfers between devices: 331 us -> none
    all_gather x7 -> x0, blocking collectives: 133 us -> none  [the longest x3 59.6 us: key_backward(): lax.all_gather(delta, 'tok', axis=1, tiled=True)]
    psum x1 -> x0, waiting for transfers between devices: 91.7 us -> none  [local(): prefix_sums = lax.psum((prefix_key_total, prefix_value_total), 'tok')]
    all_gather x24 -> x0, local copies, waits for them, and re-layouts: 73.1 us -> none  [the longest x6 23 us: attention_forward(): lax.all_gather(key_rows, 'tok', axis=0, tiled=True)]
  transfers between devices with their start and end apart: 44 -> 0, of which waited for: 30 -> 0; matrix products, arithmetic and copies ran while one was open for 25% -> 0% of each run, Pallas kernels for 0% -> 0%
where the time goes in v1:
time: 408 us; the launch traced here: 404 us
  Pallas kernels  374 us (92%)
  local copies, waits for them, and re-layouts  24 us (6%)
  other arithmetic  5.36 us (1%)
    pallas_call x1, Pallas kernels, cube_local(): pl.pallas_call(kernel, out_shape=(shape((2, ROWS, width), BF16), shape((2...  374 us
    unnamed x48, local copies, waits for them, and re-layouts  9.1 us

profile of v1, /device:TPU:0, one launch (start us, length us, event | category | flops | bytes accessed | tf_op | source)
XLA Modules:
  0.0 404.2 jit_solution(3326608797371477445)
XLA Ops:
  0.7 1.2 reshape_squeeze.13
  1.8 0.0 copy-done.6
  1.9 0.2 reshape_squeeze.14
  2.0 0.0 copy-start.7
  2.0 0.1 copy_bitcast_fusion.1
  2.2 0.8 copy-done.7
  2.9 0.2 reshape_squeeze.12
  3.1 0.1 copy.74
  3.2 0.0 copy-start.10
  3.2 0.7 copy-done.10
  3.9 0.1 reshape.94
  4.0 0.1 copy.61
  4.1 0.5 copy-done.11
  4.7 0.1 copy.53
  4.8 0.5 copy-done.12
  5.3 0.1 copy.54
  5.4 0.5 copy-done.13
  6.0 0.1 copy.55
  6.1 0.5 copy-done.14
  6.6 0.1 copy.56
  6.7 0.5 copy-done.15
  7.3 0.1 copy.57
  7.4 0.5 copy-done.16
  7.9 0.1 copy.58
  8.0 0.5 copy-done.17
  8.6 0.1 copy.59
  8.7 0.5 copy-done.18
  9.2 0.1 copy.60
  9.4 0.1 concatenate.6
  9.6 0.0 copy-start.3
  9.6 1.1 pad_maximum_fusion.wqkv_src
  10.7 0.4 reshape_squeeze.15
  11.1 0.5 copy.73
  11.6 1.1 reshape.95.wup_src
  12.7 374.0 %shard_map.339 = (bf16[2,64,1024]{2,1,0:T(8,128)(2,1)}, bf16[2,64,1024]{2,1,0:T(8,128)(2,1)}, bf16[16,64,256]{2,1,0:T(8,128)(2,1)}, bf16[16,64,256]{2,1,0:T(8,12...) custom-call(s32[2,8]{1,0:T(2,128)} %lengths.1, ...), custom_call_target="tpu_custom_call" | custom-call | tf_op jit(solution)/shard_map/pallas_call | solution.py:1428
  386.7 0.9 reduce_sum.9
  387.7 0.1 constant_dynamic-slice_fusion
  387.8 0.5 fusion.1
  388.3 0.1 copy-done.9
  388.5 0.6 dynamic-slice_bitcast_fusion
  389.0 0.5 fusion.2
  389.6 1.3 convert_bitcast_fusion.2
  390.9 0.3 copy.63
  391.2 0.9 reshape.110
  392.1 0.3 copy.64
  392.4 0.9 reshape.112
  393.2 0.3 copy.65
  393.6 0.9 reshape.114
  394.4 0.1 copy-done
  394.5 0.1 convert_bitcast_fusion
  394.7 0.3 copy.67
  395.0 0.9 reshape.120
  395.8 0.3 copy.68
  396.2 0.9 reshape.122
  397.0 0.2 copy-done.2
  397.2 0.5 reshape.130
  397.7 0.8 copy.66
  398.5 1.8 reshape.117
  400.4 1.1 bitcast_convert_fusion
  401.4 0.7 bitcast_convert_fusion.1
  402.2 0.3 copy-done.5
  402.5 0.7 copy.77
  403.2 0.3 copy-done.4
  403.5 0.7 copy.78
  (25 shorter events, 0.1 us)
Async XLA Ops:
  0.7 1.2 copy-start.6
  2.0 0.9 copy-start.7
  3.2 0.7 copy-start.10
  4.0 0.7 copy-start.11
  4.7 0.7 copy-start.12
  5.3 0.7 copy-start.13
  6.0 0.7 copy-start.14
  6.6 0.7 copy-start.15
  7.3 0.7 copy-start.16
  7.9 0.7 copy-start.17
  8.6 0.7 copy-start.18
  9.6 1.2 copy-start.3
  387.7 0.8 copy-start.9
  393.6 1.0 copy-start
  396.2 1.0 copy-start.2
  398.5 1.8 copy-start.1
  400.4 1.1 copy-start.8
  401.4 1.0 copy-start.5
  402.5 1.0 copy-start.4

commit v2 on v1

--- a/solution.py
+++ b/solution.py
@@ -564,7 +564,8 @@
 F32 = jnp.float32
 BF16 = jnp.bfloat16
 ROWS = 64
-PIECE = 32
+PIECE = 16
+PIECES = ROWS // PIECE
 BLOCK = 256
 SQRT_HALF = 0.7071067811865476
 INV_SQRT_2PI = 0.3989422804014327
@@ -638,12 +639,39 @@
         return rows_at(flip(self.x, j // 2) * 2 + flip(self.zl, j % 2), BLOCK)
 
 
+def hops_of(first, last):
+    hops = {(r, q): hop for q in range(PIECES) for r, hop in first}
+    for q, (via, step, seen) in enumerate(last):
+        hops[(via, q)] = (step, seen)
+    return hops
+
+
+class Pump:
+    def __init__(self, rate=3):
+        self.waiting = []
+        self.rate = rate
+
+    def add(self, starts):
+        self.waiting += starts
+
+    def go(self, count=None):
+        count = self.rate if count is None else count
+        for start in self.waiting[:count]:
+            start()
+        del self.waiting[:count]
+
+
 class Gather:
-    HOPS = {(1, 0): (2, 3), (1, 1): (2, 3), (2, 0): (4, 6), (2, 1): (4, 6), (4, 0): (1, 5), (4, 1): (1, 5),
-            (3, 0): (4, 7), (6, 1): (1, 7)}
-
-    def __init__(self, place, buf, recv, sib, sends):
+    CUBE = (
+        (4, 2, 1), ((1, 2, 4), (3, 6, 5), (7,)), (0, 2, 1, 3),
+        hops_of(((1, (2, 3)), (2, (4, 6)), (4, (1, 5))), ((3, 4, 7), (6, 1, 7), (5, 2, 7), (3, 4, 7))),
+    )
+    FACE = ((2, 1), ((1, 2), (3,)), (0, 1), hops_of((), ((1, 2, 3), (2, 1, 3), (1, 2, 3), (2, 1, 3))))
+
+    def __init__(self, place, buf, recv, sib, sends, face=False):
         self.place, self.buf, self.recv, self.sib, self.sends = place, buf, recv, sib, sends
+        self.near, self.stages, self.order, self.hops = self.FACE if face else self.CUBE
+        self.pump = Pump()
 
     def piece(self, r, q, other=0):
         core = flip(self.place.core, other)
@@ -651,9 +679,9 @@
         return self.buf.at[pl.ds(pl.multiple_of(row, PIECE), PIECE)]
 
     def start(self):
-        for q in range(2):
+        for q in range(PIECES):
             own = self.piece(0, q)
-            for r in (4, 2, 1):
+            for r in self.near:
                 remote(own, own, self.sends.at[0, r, q], self.recv.at[r, q], self.place.peer(r)).start()
             self.to_sibling(0, q).start()
 
@@ -664,53 +692,51 @@
     def arrive(self, r, q):
         rows = self.piece(r, q)
         bytes_of(rows, self.recv.at[r, q]).wait()
-        if (r, q) in self.HOPS:
-            self.onward(r, q).start()
+        if (r, q) in self.hops:
+            hop, seen = self.hops[(r, q)]
+            remote(rows, rows, self.sends.at[2, r, q], self.recv.at[seen, q], self.place.peer(hop)).start()
         self.to_sibling(r, q).start()
 
-    def onward(self, r, q):
-        hop, seen = self.HOPS[(r, q)]
-        rows = self.piece(r, q)
-        return remote(rows, rows, self.sends.at[2, r, q], self.recv.at[seen, q], self.place.peer(hop))
-
     def stage(self, number):
-        order = ((1, 2, 4), (3, 6, 5), (7,))[number]
-        for q in range(2):
-            for r in order:
+        for q in range(PIECES):
+            for r in self.stages[number]:
                 self.arrive(r, q)
-
-    def ready(self, r):
-        for q in range(2):
-            bytes_of(self.piece(r, q, 1), self.sib.at[r, q]).wait()
+            self.pump.go()
 
     def pair_ready(self, j):
-        self.ready(2 * j)
-        self.ready(2 * j + 1)
+        for r in (2 * j, 2 * j + 1):
+            for q in range(PIECES):
+                bytes_of(self.piece(r, q, 1), self.sib.at[r, q]).wait()
 
     def blocks(self, use):
-        for j in range(4):
-            if j < 3:
-                self.stage(j)
+        before = None
+        for i, j in enumerate(self.order):
+            if i < len(self.stages):
+                self.stage(i)
             self.pair_ready(j)
-            use(j)
+            use(j, before)
+            before = j
         self.drain()
 
     def drain(self):
-        for q in range(2):
-            own = self.piece(0, q)
-            for r in (4, 2, 1):
+        own = self.piece(0, 0)
+        for q in range(PIECES):
+            for r in self.near:
                 bytes_of(own, self.sends.at[0, r, q]).wait()
-            for r in range(8):
+            for r in range(2 * len(self.order)):
                 bytes_of(own, self.sends.at[1, r, q]).wait()
-        for r, q in self.HOPS:
-            bytes_of(self.piece(0, q), self.sends.at[2, r, q]).wait()
+        for r, q in self.hops:
+            bytes_of(own, self.sends.at[2, r, q]).wait()
 
 
 class Scatter:
+    WAY = {3: (2, (7, 0)), 6: (4, (7, 1)), 5: (1, None), 1: (1, 3), 2: (2, 6), 4: (4, 5)}
+
     def __init__(self, place, recv, sends, half, keep, sib_out, sib_in, out, inbox):
         self.place, self.recv, self.sends = place, recv, sends
         self.half, self.keep, self.sib_out, self.sib_in = half, keep, sib_out, sib_in
         self.out, self.inbox = out, inbox
+        self.pump = Pump()
 
     def pair(self, r):
         return remote(
@@ -718,8 +744,16 @@
         )
 
     def push(self, r):
+        step = self.WAY[r][0]
         return remote(
-            self.out.at[r], self.inbox.at[r], self.sends.at[1, r], self.recv.at[1, r], self.place.peer(r)
+            self.out.at[r], self.inbox.at[r], self.sends.at[1, r], self.recv.at[1, r], self.place.peer(step)
+        )
+
+    def part(self, q):
+        rows, slot = pl.ds(q * 32, 32), (7, 0)[q]
+        return remote(
+            self.out.at[7, rows], self.inbox.at[7, rows], self.sends.at[1, slot], self.recv.at[1, slot],
+            self.place.peer((4, 1)[q]),
         )
 
     def give(self, j, partial):
@@ -732,20 +766,29 @@
             self.sib_out[r] = self.half[2 * b + 1 - core].astype(BF16)
             self.pair(r).start()
 
-    def forward(self, j):
-        for k in (1, 0):
-            r = 2 * j + k
-            self.pair(r).wait_recv()
-            total = self.keep[r] + self.sib_in[r].astype(F32)
-
-            @pl.when(r == 0)
-            def _():
-                self.keep[0] = total
-
-            @pl.when(r != 0)
-            def _():
-                self.out[r] = total.astype(BF16)
-                self.push(r).start()
+    def forward(self, r):
+        self.pair(r).wait_recv()
+        if r == 7:
+            self.out[7] = (self.keep[7] + self.sib_in[7].astype(F32)).astype(BF16)
+            self.part(0).start()
+            self.part(1).start()
+            return
+        more = self.WAY[r][1]
+        if more is None:
+            self.out[r] = (self.keep[r] + self.sib_in[r].astype(F32)).astype(BF16)
+        elif isinstance(more, int):
+            self.push(more).wait_recv()
+            self.out[r] = (self.keep[r] + self.sib_in[r].astype(F32) + self.inbox[more].astype(F32)).astype(BF16)
+        else:
+            q = more[1]
+            self.part(q).wait_recv()
+            for k in range(2):
+                rows = pl.ds(k * 32, 32)
+                total = self.keep[r, rows] + self.sib_in[r, rows].astype(F32)
+                if k == q:
+                    total = total + self.inbox[7, rows].astype(F32)
+                self.out[r, rows] = total.astype(BF16)
+        self.push(r).start()
 
     def run(self, produce):
         def step(i, carry):
@@ -753,32 +796,33 @@
             def _():
                 self.give(3 - i, produce(3 - i))
 
-            @pl.when(i >= 1)
-            def _():
-                self.forward(4 - i)
+            for when, steps in ((1, (7,)), (2, (5,)), (3, (3, 6)), (4, (1, 2, 4))):
+                @pl.when(i == when)
+                def _():
+                    for r in steps:
+                        self.forward(r)
+                    self.pump.go()
 
             return carry
 
         lax.fori_loop(0, 5, step, 0)
 
+    def rest(self):
+        for r in (7, 3, 6, 1, 2, 4):
+            self.forward(r)
+
     def finish(self):
-        def collect(r, carry):
+        self.pair(0).wait_recv()
+        self.keep[0] = self.keep[0] + self.sib_in[0].astype(F32)
+        for r in (1, 2, 4):
             self.push(r).wait_recv()
             self.keep[0] = self.keep[0] + self.inbox[r].astype(F32)
-            return carry
-
-        lax.fori_loop(1, 8, collect, 0)
-
-        def drain(r, carry):
+        for r in range(8):
             self.pair(r).wait_send()
-
-            @pl.when(r >= 1)
-            def _():
-                self.push(r).wait_send()
-
-            return carry
-
-        lax.fori_loop(0, 8, drain, 0)
+        for r in self.WAY:
+            self.push(r).wait_send()
+        for q in range(2):
+            self.part(q).wait_send()
         return self.keep[0]
 
 
@@ -807,10 +851,12 @@
 
 
 def kernel(
-    lengths, inputs, cotangent, wqkv_src, wup_src, wdn_src, wout_src, pk_src, pv_src,
+    lengths, inputs, cotangent, wq_src, wk_src, wv_src, wup_src, wdn_src, wout_src, pk_src, pv_src,
+    v0, v1, v2, v3, v4, v5, v6, v7, v8,
     out_y, out_dx, got_qkv, got_up, got_dn, got_out, got_prefix, got_rows, got_bias,
     ag_recv, ag_sib, ag_send, rs_recv, rs_send,
-    wsend, wown, wtwin, wrelay, psem, xsem, osend, orecv, tsend, trecv, gsend, grecv,
+    wsend, wown, wtwin, wrelay, psem, xsem, osend, orecv, tsend, trecv, gsend, grecv, rsem,
+    raw_qkv, raw_up, pack_qkv, pack_up, vrows, u0, u1, u2, u3, u4, u5, u6, u7, u8,
     wqkv, wup, wdn, wout, pre,
     qseg, kseg, xg, ng, dzg, dog, param,
     qs, ks, vs, kt, vt, lse, ctb, ctf,
@@ -838,48 +884,106 @@
         return carry
 
     lax.fori_loop(0, 32, greet, 0)
+
+    raw = [local_copy(src.at[0], raw_qkv.at[i], rsem.at[i]) for i, src in enumerate((wq_src, wk_src, wv_src))]
+    raw.append(local_copy(wup_src.at[0], raw_up, rsem.at[3]))
+    vectors = (u0, u1, u2, u3, u4, u5, u6, u7, u8)
+    for i, (src, dst) in enumerate(zip((v0, v1, v2, v3, v4, v5, v6, v7, v8), vectors)):
+        raw.append(local_copy(src, dst, rsem.at[4 + i]))
+    for copy in raw:
+        copy.start()
+    vrows[...] = jnp.zeros_like(vrows)
+    for copy in raw:
+        copy.wait()
+    for i in range(8):
+        vrows[i : i + 1, 0:64] = vectors[i][...].astype(F32)
+    up_row = u8[...].astype(F32)
+    for i in range(4):
+        vrows[8 + i : 9 + i, 0:64] = up_row[:, i * 64 : (i + 1) * 64]
+    vector_columns = vrows[...].T[0:64]
+
+    def pack_heads(h, carry):
+        cols = rows_at(h, 128)
+        parts = [raw_qkv[i, :, cols].astype(F32) for i in range(3)]
+        for s in range(2):
+            sides = [part[:, s * 64 : (s + 1) * 64] for part in parts]
+            pack_qkv[2 * h + s] = jnp.concatenate(sides + [vector_columns], axis=1).astype(BF16)
+        return carry
+
+    lax.fori_loop(0, 8, pack_heads, 0)
+    for side in range(2):
+        for rest in range(8):
+            for zhi in range(2):
+                start = (zhi * 8 + rest) * 256 + side * 128
+                pack_up[side * 8 + rest, :, zhi * 128 : (zhi + 1) * 128] = raw_up[:, start : start + 128]
+
     pl.semaphore_wait(barrier, 31)
 
     own_rows = rows_at(tau, ROWS)
-    x_here = local_copy(inputs.at[cube], xg.at[0, own_rows], xsem.at[0])
-    x_there = remote(inputs.at[1 - cube], xg.at[0, own_rows], xsem.at[1], xsem.at[2], place.twin())
-    d_here = local_copy(cotangent.at[cube], dstage.at[2], xsem.at[3])
-    d_there = remote(cotangent.at[1 - cube], dstage.at[2], xsem.at[4], xsem.at[5], place.twin())
-
-    @pl.when(x == cube)
-    def _():
-        x_there.start()
-        x_here.start()
-
-    def spread_out(kind):
-        src_all, dst_all = ((wqkv_src, wqkv), (wup_src, wup))[kind]
-
-        def one(k, carry):
+    first, last = pl.ds(0, 32), pl.ds(32, 32)
+    diagonal = place.device(1 - x, 1 - cube)
+    neighbour = place.device(1 - x, cube)
+
+    def shares(source, target, far, sem):
+        here = local_copy(source.at[cube], target, xsem.at[sem])
+        to_twin = remote(source.at[1 - cube, first], target.at[first], xsem.at[sem + 1], xsem.at[sem + 2], place.twin())
+        to_diagonal = remote(source.at[1 - cube, last], far.at[last], xsem.at[sem + 1], xsem.at[sem + 3], diagonal)
+
+        def start():
+            @pl.when(x == cube)
+            def _():
+                to_twin.start()
+                here.start()
+
+            pl.when(x != cube)(to_diagonal.start)
+
+        def arrived():
+            @pl.when(x != cube)
+            def _():
+                to_twin.wait_recv()
+                to_diagonal.wait_recv()
+
+            pl.when(x == cube)(here.wait)
+
+        def sent():
+            pl.when(x == cube)(to_twin.wait_send)
+            pl.when(x != cube)(to_diagonal.wait_send)
+
+        return start, arrived, sent
+
+    x_start, x_arrived, x_sent = shares(inputs, xg.at[0, own_rows], xg.at[0, rows_at(tau + 8 - 16 * x, ROWS)], 0)
+    d_start, d_arrived, d_sent = shares(cotangent, dstage.at[2], dstage.at[2], 4)
+    x_start()
+
+    def spread_pushes(kind):
+        src_all, dst_all = (pack_qkv, pack_up)[kind], (wqkv, wup)[kind]
+        dst, sem = dst_all.at[rows_at(x * 16 + t, ROWS)], wown.at[kind, x, t % 8]
+        for k in range(16):
             to = lax.rem(k + tau + 1, 16)
-            src, dst = src_all.at[to], dst_all.at[rows_at(x * 16 + t, ROWS)]
-            sem = wown.at[kind, x, t % 8]
-
-            @pl.when(to == tau)
-            def _():
-                local_copy(src, dst, sem).start()
-
-            @pl.when(to != tau)
-            def _():
-                remote(src, dst, wsend.at[kind], sem, (to // 8, cube * 8 + to % 8)).start()
-
-            return carry
-
-        lax.fori_loop(0, 16, one, 0)
-
-    def slices_out():
-        for side in range(2):
-            src = wdn_src.at[0, pl.ds(side * 128, 128)]
-            dst = wdn.at[x, rows_at(cube, 128)]
-            pl.when(x == side)(local_copy(src, dst, wown.at[3, x, 0]).start)
-            pl.when(x != side)(remote(src, dst, wsend.at[3], wown.at[3, x, 0], place.device(1 - x, cube)).start)
-        src, dst = wout_src.at[0], wout.at[x]
-        pl.when(x == cube)(local_copy(src, dst, wown.at[2, x, 0]).start)
-        pl.when(x != cube)(remote(src, dst, wsend.at[2], wown.at[2, x, 0], place.device(1 - x, cube)).start)
+
+            def go(to=to):
+                src = src_all.at[to]
+                pl.when(to == tau)(local_copy(src, dst, sem).start)
+                pl.when(to != tau)(remote(src, dst, wsend.at[kind], sem, (to // 8, cube * 8 + to % 8)).start)
+
+            yield go
+
+    def slice_pushes():
+        neighbour = place.device(1 - x, cube)
+
+        def give_out():
+            src, dst = wout_src.at[0], wout.at[x]
+            pl.when(x == cube)(local_copy(src, dst, wown.at[2, x, 0]).start)
+            pl.when(x != cube)(remote(src, dst, wsend.at[2], wown.at[2, x, 0], neighbour).start)
+
+        def give_down():
+            for side in range(2):
+                src = wdn_src.at[0, pl.ds(side * 128, 128)]
+                dst = wdn.at[x, rows_at(cube, 128)]
+                pl.when(x == side)(local_copy(src, dst, wown.at[3, x, 0]).start)
+                pl.when(x != side)(remote(src, dst, wsend.at[3], wown.at[3, x, 0], neighbour).start)
+
+        return give_out, give_down
 
     def prefix_out():
         for side, index in ((x, 0), (1 - x, 1)):
@@ -891,58 +995,53 @@
                 else:
                     yield remote(src, dst, psem.at[1, kind], psem.at[2, kind], place.device(1 - x, cube))
 
-    def twin_copy(kind, l):
+    def slice_ref(kind, l, zhi):
         if kind < 2:
-            ref = (wqkv, wup)[kind].at[rows_at(l * 2 + cube, half_rows)]
-        elif kind == 3:
-            ref = wdn.at[l, rows_at(cube, 128)]
-        else:
-            ref = wout.at[l]
+            return (wqkv, wup)[kind].at[rows_at(l * 2 + zhi, half_rows)]
+        if kind == 3:
+            return wdn.at[l, rows_at(zhi, 128)]
+        return wout.at[l]
+
+    def to_twin(ref, kind, l):
         return remote(ref, ref, wrelay.at[kind, l], wtwin.at[kind, l], place.twin())
 
     def relay_blocks(kind, l):
-        ref_all = (wqkv, wup)[kind]
-
-        def one(k, carry):
-            ref = ref_all.at[rows_at((l * 2 + cube) * 8 + k, ROWS)]
+        def one(i, carry):
+            k = lax.rem(jnp.where(x == l, tau, 0) + 7 - i, 8)
+            ref = (wqkv, wup)[kind].at[rows_at((l * 2 + cube) * 8 + k, ROWS)]
             bytes_of(ref, wown.at[kind, l, k]).wait()
-            remote(ref, ref, wrelay.at[kind, l], wtwin.at[kind, l], place.twin()).start()
+            to_twin(ref, kind, l).start()
             return carry
 
         lax.fori_loop(0, 8, one, 0)
 
-    def relay_slices(l):
-        dn = wdn.at[l, rows_at(cube, 128)]
-        bytes_of(dn, wown.at[3, l, 0]).wait()
-        twin_copy(3, l).start()
-
+    def relay_out(l):
         @pl.when(x == cube)
         def _():
             bytes_of(wout.at[l], wown.at[2, l, 0]).wait()
-            twin_copy(2, l).start()
+            to_twin(wout.at[l], 2, l).start()
+
+    def relay_down(l):
+        dn = slice_ref(3, l, cube)
+        bytes_of(dn, wown.at[3, l, 0]).wait()
+        to_twin(dn, 3, l).start()
 
     def weights_in(kind, l):
-        if kind < 2:
-            ref = (wqkv, wup)[kind].at[rows_at(l * 2 + 1 - cube, half_rows)]
-        elif kind == 3:
-            ref = wdn.at[l, rows_at(1 - cube, 128)]
-        else:
-            ref = wout.at[l]
-        wait = bytes_of(ref, wtwin.at[kind, l]).wait
+        wait = bytes_of(slice_ref(kind, l, 1 - cube), wtwin.at[kind, l]).wait
         if kind == 2:
             pl.when(x != cube)(wait)
         else:
             wait()
 
     def weights_drain():
-        for kind, ref in ((0, wqkv), (1, wup)):
-            bytes_of(ref.at[pl.ds(0, 15 * ROWS)], wsend.at[kind]).wait()
+        for kind, ref in ((0, pack_qkv), (1, pack_up)):
+            bytes_of(ref.at[pl.ds(0, 15)], wsend.at[kind]).wait()
         bytes_of(wdn.at[0, pl.ds(0, 128)], wsend.at[3]).wait()
         pl.when(x != cube)(bytes_of(wout.at[0], wsend.at[2]).wait)
         for l in range(2):
             for kind in (0, 1, 3):
-                twin_copy(kind, l).wait_send()
-            pl.when(x == cube)(twin_copy(2, l).wait_send)
+                to_twin(slice_ref(kind, l, cube), kind, l).wait_send()
+            pl.when(x == cube)(to_twin(wout.at[l], 2, l).wait_send)
 
     def weight(ref, l):
         return ref[rows_at(l, 16 * ROWS)]
@@ -956,7 +1055,7 @@
     def scatter(phase):
         boxes = phase % 2
         return Scatter(
-            place, rs_recv.at[phase], rs_send, half, keep, sib_out, sib_in.at[boxes], rs_out, inbox.at[boxes]
+            place, rs_recv.at[phase], rs_send, half, keep, sib_out, sib_in.at[boxes], rs_out, inbox.at[boxes],
         )
 
     prefixes = list(prefix_out())
@@ -965,7 +1064,8 @@
 
     @pl.when(x == 0)
     def _():
-        spread_out(0)
+        for start in spread_pushes(0):
+            start()
 
     rowacc[...] = jnp.zeros_like(rowacc)
     biasacc[...] = jnp.zeros_like(biasacc)
@@ -982,8 +1082,8 @@
     kseg[0:tokens] = segment_k
     kseg[tokens:] = jnp.full((kseg.shape[0] - tokens, 128), -1, jnp.int32)
 
-    pl.when(x != cube)(x_there.wait_recv)
-    pl.when(x == cube)(x_here.wait)
+    relay_blocks(0, 0)
+    x_arrived()
 
     def result_out(stage, out, kind, layer):
         dst = out.at[cube]
@@ -1003,19 +1103,20 @@
 
         @pl.when(l == 0)
         def _():
-            @pl.when(x == 0)
-            def _():
-                spread_out(1)
-                slices_out()
-
-            @pl.when(x == cube)
-            def _():
-                d_there.start()
-                d_here.start()
-
-            for number in range(3):
-                gather_x.stage(number)
-            relay_blocks(0, 0)
+            def first_layer(start):
+                return lambda: pl.when(x == 0)(start)
+
+            give_out, give_down = slice_pushes()
+            gather_x.pump.add([first_layer(start) for start in (give_out, *spread_pushes(1), give_down)])
+            gather_x.stage(0)
+            gather_x.pump.go(1)
+            relay_out(0)
+            gather_x.stage(1)
+            relay_blocks(1, 0)
+            gather_x.pump.go(len(gather_x.pump.waiting))
+            gather_x.stage(2)
+            relay_down(0)
+            d_start()
             for copy in prefixes[:2]:
                 copy.wait()
             for copy in prefixes[2:]:
@@ -1036,11 +1137,11 @@
         kt[l, :, tokens:] = prefix_t[:64].astype(BF16)
         vt[l, :, tokens:] = prefix_t[64:].astype(BF16)
 
-        for j in range(4):
-            if j < 3:
+        for i, j in enumerate(gather_x.order):
+            if i < 3:
                 @pl.when(l == 1)
                 def _():
-                    gather_x.stage(j)
+                    gather_x.stage(i)
 
             gather_x.pair_ready(j)
             rows = place.pair_rows(j)
@@ -1053,18 +1154,15 @@
             vt[l, :, rows] = value_t[128:192].astype(BF16)
         gather_x.drain()
 
-        @pl.when(l == 0)
-        def _():
-            relay_slices(0)
-            relay_blocks(1, 0)
-
-            @pl.when(x == 1)
-            def _():
-                spread_out(0)
-                slices_out()
-                spread_out(1)
-
+        def second_layer(start):
+            return lambda: pl.when((l == 0) & (x == 1))(start)
+
+        give_out, give_down = slice_pushes()
         scatter_o = scatter(RS_O)
+        scatter_o.pump = Pump(9)
+        scatter_o.pump.add(
+            [second_layer(start) for start in (*spread_pushes(0), give_out, give_down, *spread_pushes(1))]
+        )
 
         def attend(j):
             cols = place.pair_rows(j)
@@ -1106,7 +1204,7 @@
         up_bias = jnp.concatenate([up_parts[0:1], up_parts[1:2], up_more[0:1], up_more[1:2]], axis=1)
         scatter_z = scatter(RS_Z)
 
-        def feed_block(j):
+        def feed_block(j, before):
             rows = place.pair_rows(j)
             value = mm(ng[l, rows], weight(wup, l)) + up_bias
             cdf = 0.5 * (1.0 + lax.erf(value * SQRT_HALF))
@@ -1114,16 +1212,17 @@
             act[l, rows] = low
             dact[l, rows] = cdf + value * (jnp.exp(-0.5 * value * value) * INV_SQRT_2PI)
             scatter_z.give(j, mm(low, wdn[l]))
-            if j:
-                scatter_z.forward(j - 1)
+            if j == 1:
+                scatter_z.forward(5)
 
         gather_n.blocks(feed_block)
-        scatter_z.forward(3)
+        scatter_z.rest()
 
         @pl.when(l == 0)
         def _():
-            relay_slices(1)
+            relay_out(1)
             relay_blocks(1, 1)
+            relay_down(1)
 
         mixed = scatter_z.finish() + param[l, 3:4]
         result = norm_forward(
@@ -1142,15 +1241,15 @@
 
     lax.fori_loop(0, 2, forward_layer, 0)
 
-    pl.when(x != cube)(d_there.wait_recv)
-    pl.when(x == cube)(d_here.wait)
+    d_arrived()
 
     other_half, this_half = 1 - cube, cube
 
     def twin_parts(kind, l):
-        if kind < 2:
-            ref, box = ((g_qkv, t_qkv), (g_up, t_up))[kind]
-            return ref.at[l, rows_at(other_half, half_rows)], box, ref.at[l, rows_at(this_half, half_rows)]
+        if kind == 0:
+            return g_qkv.at[l, rows_at(other_half, half_rows)], t_qkv, g_qkv.at[l, rows_at(this_half, half_rows)]
+        if kind == 1:
+            return g_up.at[l, rows_at(other_half, half_rows)], t_up, g_up.at[l, rows_at(this_half, half_rows)]
         if kind == 2:
             return g_prefix.at[l, rows_at(other_half, 32)], t_prefix, g_prefix.at[l, rows_at(this_half, 32)]
         if kind == 3:
@@ -1160,6 +1259,15 @@
     def twin_send(kind, l):
         src, box, own = twin_parts(kind, l)
         return remote(src, box.at[l], tsend.at[kind, l], trecv.at[kind, l], place.twin())
+
+    def twin_chunks(kind, l):
+        src, box, own = twin_parts(kind, l)
+        rows = ROWS if kind < 2 else 16
+        for k in range(src.shape[0] // rows):
+            part = pl.ds(k * rows, rows)
+            yield remote(
+                src.at[part], box.at[l, part], tsend.at[kind, l], trecv.at[kind, l], place.twin()
+            ).start
 
     def twin_start(kind, l):
         copy = twin_send(kind, l)
@@ -1168,44 +1276,34 @@
         else:
             copy.start()
 
-    def owner_copies(kind, l, act_on):
+    def owner_pushes(kind, l):
         src, box, own = twin_parts(kind, l)
         mine = x == l
+
+        def start(is_self, part, dst, dev, condition=None):
+            def go():
+                pl.when(is_self)(local_copy(part, dst, grecv.at[kind]).start)
+                pl.when(jnp.logical_not(is_self))(
+                    remote(part, dst, gsend.at[kind, l], grecv.at[kind], dev).start
+                )
+
+            return go if condition is None else lambda: pl.when(condition)(go)
+
         if kind < 2:
             got = (got_qkv, got_up)[kind]
-
-            def one(k, carry):
+            for k in range(8):
                 to = lax.rem(k + t + 1, 8)
-                src, dst = own.at[rows_at(to, ROWS)], got.at[tau]
-                is_self = mine & (to == t % 8)
-                act_on(is_self, src, dst, (l, cube * 8 + to))
-                return carry
-
-            lax.fori_loop(0, 8, one, 0)
+                yield start(mine & (to == t % 8), own.at[rows_at(to, ROWS)], got.at[tau], (l, cube * 8 + to))
         elif kind == 2:
-
-            def one(k, carry):
+            for k in range(16):
                 to = lax.rem(k + t + 1, 16)
-                act_on(mine & (to == t), own, got_prefix.at[tau, rows_at(this_half, 32)], (l, to))
-                return carry
-
-            lax.fori_loop(0, 16, one, 0)
+                yield start(mine & (to == t), own, got_prefix.at[tau, rows_at(this_half, 32)], (l, to))
         elif kind == 3:
-            act_on(mine, own, got_dn.at[rows_at(x, 128)], place.device(l, cube))
+            yield start(mine, own, got_dn.at[rows_at(x, 128)], place.device(l, cube))
         else:
-
-            @pl.when(x == cube)
-            def _():
-                act_on(mine, own, got_out, place.device(l, cube))
-
-    def start_on(kind, l):
-        def act_on(is_self, src, dst, dev):
-            pl.when(is_self)(local_copy(src, dst, grecv.at[kind]).start)
-            pl.when(jnp.logical_not(is_self))(remote(src, dst, gsend.at[kind, l], grecv.at[kind], dev).start)
-
-        return act_on
-
-    def owner_start(kind, l):
+            yield start(mine, own, got_out, place.device(l, cube), x == cube)
+
+    def owner_add(kind, l):
         src, box, own = twin_parts(kind, l)
 
         def add():
@@ -1216,7 +1314,11 @@
             pl.when(x == cube)(add)
         else:
             add()
-        owner_copies(kind, l, start_on(kind, l))
+
+    def owner_start(kind, l):
+        owner_add(kind, l)
+        for start in owner_pushes(kind, l):
+            start()
 
     def grads_drain(l):
         for kind in range(5):
@@ -1273,16 +1375,16 @@
         rowacc[l, 5:6] = column_sum(low)
         scatter_n = scatter(RS_N)
 
-        def back_block(j):
+        def back_block(j, before):
             rows = place.pair_rows(j)
             low = (dact[l, rows] * mm_nt(dzg[rows], wdn[l])).astype(BF16)
             dfs[rows] = low
             scatter_n.give(j, mm_nt(low, weight(wup, l)))
-            if j:
-                scatter_n.forward(j - 1)
+            if j == 1:
+                scatter_n.forward(5)
 
         gather_z.blocks(back_block)
-        scatter_n.forward(3)
+        scatter_n.rest()
         biasacc[l, 1:2] = column_sum(dfs[...])
 
         def down_tile(i, carry):
@@ -1298,13 +1400,20 @@
             return carry
 
         lax.fori_loop(0, width // 256, up_tile, 0)
-        twin_start(3, l)
-        twin_start(1, l)
-
-        @pl.when(step == 1)
+        @pl.when(l == 0)
         def _():
-            owner_start(0, 1)
-            owner_start(4, 1)
+            for kind in (3, 1, 2, 4, 0):
+                owner_add(kind, 1)
+
+        def older(start):
+            return lambda: pl.when(l == 0)(start)
+
+        pump = Pump()
+        twins = [*twin_chunks(3, l), *twin_chunks(1, l)]
+        olds = [older(start) for kind in (3, 1, 4, 0, 2) for start in owner_pushes(kind, 1)]
+        for k in range(17):
+            pump.add(twins[k : k + 1] + olds[2 * k : 2 * k + 2])
+        pump.go(3)
 
         d_normal = own_b[...] + scatter_n.finish()
         d_sum, d_gain, d_shift = norm_backward(d_normal, param[l, 1:2], hat1.at[l], rstd1.at[l])
@@ -1312,15 +1421,18 @@
         low = d_sum.astype(BF16)
         dog[own_rows] = low
         gather_o = gather(dog, AG_O)
+        gather_o.pump = pump
         gather_o.start()
         rowacc[l, 0:1] = d_gain
         rowacc[l, 1:2] = d_shift
         rowacc[l, 2:3] = column_sum(low)
         rows_start(l)
+
+
         dkacc[...] = jnp.zeros_like(dkacc)
         dvacc[...] = jnp.zeros_like(dvacc)
 
-        def attend_back(j):
+        def attend_back(j, before):
             cols = place.pair_rows(j)
             d_context = mm_nt(dog[cols], wout[l]).astype(BF16)
             dcb[cols] = d_context
@@ -1333,38 +1445,47 @@
             dvacc[...] += mm(probs.astype(BF16), d_context)
             dkacc[...] += mm(d_scores, qs[l, cols])
             dqt[0:64, cols] = mm(kt[l], d_scores) * 0.125
+            pump.go(3)
 
         gather_o.blocks(attend_back)
         g_prefix[l] = jnp.concatenate([dkacc[tokens:], dvacc[tokens:]], axis=1).astype(BF16)
         twin_start(2, l)
-        scatter_x = scatter(RS_X)
-
-        def assemble(j):
-            rows = place.pair_rows(j)
+        g_out[l] = mm(ctb[l], dog[...]).astype(BF16)
+        twin_start(4, l)
+
+        def assemble(i, carry):
+            rows = rows_at(i, BLOCK)
             d_query = dqt[:, rows].T[:, :64]
             value = jnp.concatenate(
                 [d_query, dkacc[rows], dvacc[rows], jnp.zeros((BLOCK, 64), F32)], axis=1
             )
-            low = value.astype(BF16)
-            dqkv[rows] = low
+            dqkv[rows] = value.astype(BF16)
             dqkvt[:, rows] = value.T.astype(BF16)
-            return mm_nt(low, weight(wqkv, l))
-
-        scatter_x.run(assemble)
-        biasacc[l, 0:1] = column_sum(dqkv[...])
-        bias_start(l)
+            return carry
+
+        lax.fori_loop(0, tokens // BLOCK, assemble, 0)
 
         def qkv_tile(i, carry):
             cols = rows_at(i, 256)
             g_qkv[l, cols] = mm(dqkvt[...], xg[l, :, cols]).T.astype(BF16)
             return carry
 
-        lax.fori_loop(0, width // 256, qkv_tile, 0)
-        twin_start(0, l)
-        g_out[l] = mm(ctb[l], dog[...]).astype(BF16)
-        twin_start(4, l)
-        for kind in (3, 1, 2):
-            owner_start(kind, l)
+        lax.fori_loop(other_half * 2, other_half * 2 + 2, qkv_tile, 0)
+        pump.add(list(twin_chunks(0, l)))
+        pump.go(2)
+        scatter_x = scatter(RS_X)
+        scatter_x.pump = pump
+        pump.rate = 2
+        scatter_x.run(lambda j: mm_nt(dqkv[place.pair_rows(j)], weight(wqkv, l)))
+        biasacc[l, 0:1, 0:256] = column_sum(dqkv[...])
+        bias_start(l)
+        lax.fori_loop(this_half * 2, this_half * 2 + 2, qkv_tile, 0)
+        pump.go(len(pump.waiting))
+
+        @pl.when(l == 0)
+        def _():
+            for kind in (3, 1):
+                owner_start(kind, 0)
 
         dstage[l] = (own_a[...] + scatter_x.finish()).astype(BF16)
         is_self, here, there = result_out(dstage.at[l], out_dx, 1, l)
@@ -1373,14 +1494,11 @@
         return carry
 
     lax.fori_loop(0, 2, backward_layer, 0)
-    owner_start(0, 0)
-    owner_start(4, 0)
-
-    @pl.when(x == cube)
-    def _():
-        x_there.wait_send()
-        d_there.wait_send()
-
+    for kind in (2, 4, 0):
+        owner_start(kind, 0)
+
+    x_sent()
+    d_sent()
     weights_drain()
     for l in range(2):
         grads_drain(l)
@@ -1407,18 +1525,6 @@
     keys = tokens + prefix
     hidden = b_up.shape[1]
 
-    def by_head(value):
-        return value[0].reshape(rows, heads, HEAD).transpose(1, 0, 2)
-
-    vectors = jnp.concatenate(
-        [b_out, norm1_gain, norm1_shift, b_down, norm2_gain, norm2_shift, b_query, b_value,
-         b_up.reshape(4, HEAD), jnp.zeros((HEAD - 12, HEAD), BF16)], axis=0,
-    ).T
-    wqkv_src = jnp.concatenate(
-        [by_head(w_query), by_head(w_key), by_head(w_value),
-         jnp.broadcast_to(vectors[None], (heads, rows, HEAD))], axis=-1,
-    )
-    wup_src = w_up[0].reshape(rows, 2, 8, 2, 128).transpose(3, 2, 0, 1, 4).reshape(heads, rows, 256)
     anywhere = pl.BlockSpec(memory_space=pl.ANY)
     smem = pl.BlockSpec(memory_space=pltpu.SMEM)
     dma = pltpu.SemaphoreType.DMA
@@ -1431,14 +1537,17 @@
             shape((2, ROWS, width), BF16), shape((2, ROWS, width), BF16),
             shape((16, ROWS, 256), BF16), shape((16, ROWS, 256), BF16),
             shape((hidden, width), BF16), shape((ROWS, width), BF16),
-            shape((16, prefix, 128), BF16), shape((32, 8, 128), F32), shape((4, 8, 256), F32),
+            shape((16, prefix, 128), BF16), shape((32, 8, 128), F32), shape((4, 8, hidden), F32),
         ),
-        in_specs=[smem] + [anywhere] * 8,
+        in_specs=[smem] + [anywhere] * 19,
         out_specs=[anywhere] * 9,
         scratch_shapes=[
-            dma((4, 8, 2)), dma((4, 8, 2)), dma((3, 8, 2)), dma((4, 2, 8)), dma((2, 8)),
-            dma((4,)), dma((4, 2, 8)), dma((4, 2)), dma((4, 2)), dma((3, 2)), dma((6,)),
-            dma((2, 2)), dma((2, 2)), dma((5, 2)), dma((5, 2)), dma((8, 2)), dma((7,)),
+            dma((4, 8, PIECES)), dma((4, 8, PIECES)), dma((3, 8, PIECES)), dma((4, 2, 8)), dma((2, 8)),
+            dma((4,)), dma((4, 2, 8)), dma((4, 2)), dma((4, 2)), dma((3, 2)), dma((8,)),
+            dma((2, 2)), dma((2, 2)), dma((5, 2)), dma((5, 2)), dma((8, 2)), dma((7,)), dma((13,)),
+            V((3, rows, width), BF16), V((rows, 4 * width), BF16), V((heads, rows, 256), BF16), V((heads, rows, 256), BF16),
+            V((64, 128), F32),
+            *[V((1, rows), BF16)] * 8, V((1, hidden), BF16),
             V((L * 1024, 256), BF16), V((L * 1024, 256), BF16), V((L, hidden, width), BF16),
             V((L, ROWS, width), BF16), V((L, 2, prefix, 128), BF16),
             V((8, tokens), jnp.int32), V((keys, 128), jnp.int32),
@@ -1454,8 +1563,8 @@
             V((ROWS, width), F32), V((ROWS, width), F32), V((L, ROWS, width), BF16), V((L + 1, ROWS, width), BF16),
             V((tokens, hidden), BF16), V((tokens, HEAD), BF16), V((8, tokens), F32), V((128, tokens), F32),
             V((keys, HEAD), F32), V((keys, HEAD), F32), V((tokens, 256), BF16), V((256, tokens), BF16),
-            V((L, 8, width), F32), V((L, 8, 256), F32),
-            V((L, width, 256), BF16), V((L, width, 256), BF16), V((L, hidden, width), BF16),
+            V((L, 8, width), F32), V((L, 8, hidden), F32),
+            V((L, width, 256), BF16), V((L, width, hidden), BF16), V((L, hidden, width), BF16),
             V((L, ROWS, width), BF16), V((L, prefix, 128), BF16),
             V((L, width // 2, 256), BF16), V((L, width // 2, 256), BF16), V((L, hidden // 2, width), BF16),
             V((L, ROWS, width), BF16), V((L, prefix // 2, 128), BF16),
@@ -1463,7 +1572,10 @@
         compiler_params=pltpu.CompilerParams(
             collective_id=0, has_side_effects=True, vmem_limit_bytes=60 * 2**20
         ),
-    )(lengths, inputs, cotangent, wqkv_src, wup_src, w_down, w_out, prefix_keys, prefix_values)
+    )(
+        lengths, inputs, cotangent, w_query, w_key, w_value, w_up, w_down, w_out, prefix_keys, prefix_values,
+        b_out, norm1_gain, norm1_shift, b_down, norm2_gain, norm2_shift, b_query, b_value, b_up,
+    )
     out_y, out_dx, got_qkv, got_up, got_dn, got_out, got_prefix, got_rows, got_bias = results
 
     def side_by_side(value):
@@ -1472,9 +1584,9 @@
     up = got_up.reshape(2, 8, rows, 2, 128).transpose(2, 3, 1, 0, 4).astype(F32)
     row_sum = lax.dynamic_slice_in_dim(jnp.sum(got_rows, axis=0), (t % 2) * 64, 64, 1)
     side = t // 8
-    bias = got_bias[:2] + got_bias[2:]
-    bias_up = lax.dynamic_slice_in_dim(bias[:, 1], side * 128, 128, 1).reshape(1, hidden)
-    bias_qkv = lax.dynamic_index_in_dim(bias[:, 0], side, 0, keepdims=True)
+    bias_up = (got_bias[:2, 1] + got_bias[2:, 1]).reshape(2, 2, 128)
+    bias_up = lax.dynamic_index_in_dim(bias_up, side, 1, keepdims=False).reshape(1, hidden)
+    bias_qkv = lax.dynamic_index_in_dim(got_bias[:2, 0] + got_bias[2:, 0], side, 0, keepdims=True)
     return (
         out_y[None],
         out_dx[None],

time: 408 us -> 389 us (0.953)
  local copies, waits for them, and re-layouts: 24 us -> 12.5 us
    unnamed x48 -> x12, local copies, waits for them, and re-layouts: 9.1 us -> 2.23 us
    pallas_call x1, Pallas kernels: 374 us -> 370 us  [cube_local(): pl.pallas_call(kernel, out_shape=(shape((2, ROWS, width), BF16), shape((2...]
where the time goes in v2:
time: 389 us; the launch traced here: 388 us
  Pallas kernels  370 us (95%)
  local copies, waits for them, and re-layouts  12.5 us (3%)
  other arithmetic  5.14 us (1%)
    pallas_call x1, Pallas kernels, cube_local(): pl.pallas_call(kernel, out_shape=(shape((2, ROWS, width), BF16), shape((2...  370 us

profile of v2, /device:TPU:0, one launch (start us, length us, event | category | flops | bytes accessed | tf_op | source)
XLA Modules:
  0.0 388.1 jit_solution(3988071404991074698)
XLA Ops:
  0.7 369.7 %shard_map.339 = (bf16[2,64,1024]{2,1,0:T(8,128)(2,1)}, bf16[2,64,1024]{2,1,0:T(8,128)(2,1)}, bf16[16,64,256]{2,1,0:T(8,128)(2,1)}, bf16[16,64,256]{2,1,0:T(8,12...) custom-call(s32[2,8]{1,0:T(2,128)} %lengths.1, ...), custom_call_target="tpu_custom_call" | custom-call | tf_op jit(solution)/shard_map/pallas_call | solution.py:1534
  370.4 0.8 slice_add_fusion
  371.3 0.9 reduce_sum.9
  372.2 0.1 constant_dynamic-slice_fusion
  372.3 0.5 fusion.1
  372.8 0.6 dynamic-slice_bitcast_fusion
  373.4 1.6 convert_bitcast_fusion
  375.0 0.3 copy.40
  375.3 0.9 reshape.105
  376.2 0.3 copy.41
  376.5 0.9 reshape.107
  377.4 0.3 copy.42
  377.7 0.9 reshape.109
  378.6 0.3 copy.44
  378.9 0.9 reshape.115
  379.8 0.3 copy.45
  380.1 0.0 copy-start.1
  380.1 0.9 reshape.117
  381.0 0.2 copy-done.1
  381.1 0.5 reshape.125
  381.6 0.8 copy.43
  382.4 0.0 copy-start
  382.4 1.8 reshape.112
  384.3 0.0 copy-done
  384.3 0.0 copy-start.4
  384.3 1.1 bitcast_convert_fusion
  385.3 0.0 copy-start.3
  385.4 0.0 copy-done.4
  385.4 0.7 bitcast_convert_fusion.1
  386.1 0.3 copy-done.3
  386.4 0.0 copy-start.2
  386.4 0.7 copy.48
  387.1 0.3 copy-done.2
  387.4 0.7 copy.49
  (1 shorter events, 0.0 us)
Async XLA Ops:
  380.1 1.0 copy-start.1
  382.4 1.8 copy-start
  384.3 1.1 copy-start.4
  385.3 1.0 copy-start.3
  386.4 1.0 copy-start.2

commit v3 on v2

--- a/solution.py
+++ b/solution.py
@@ -647,7 +647,7 @@
 
 
 class Pump:
-    def __init__(self, rate=3):
+    def __init__(self, rate=2):
         self.waiting = []
         self.rate = rate
 
@@ -666,11 +666,10 @@
         (4, 2, 1), ((1, 2, 4), (3, 6, 5), (7,)), (0, 2, 1, 3),
         hops_of(((1, (2, 3)), (2, (4, 6)), (4, (1, 5))), ((3, 4, 7), (6, 1, 7), (5, 2, 7), (3, 4, 7))),
     )
-    FACE = ((2, 1), ((1, 2), (3,)), (0, 1), hops_of((), ((1, 2, 3), (2, 1, 3), (1, 2, 3), (2, 1, 3))))
-
-    def __init__(self, place, buf, recv, sib, sends, face=False):
+
+    def __init__(self, place, buf, recv, sib, sends):
         self.place, self.buf, self.recv, self.sib, self.sends = place, buf, recv, sib, sends
-        self.near, self.stages, self.order, self.hops = self.FACE if face else self.CUBE
+        self.near, self.stages, self.order, self.hops = self.CUBE
         self.pump = Pump()
 
     def piece(self, r, q, other=0):
@@ -853,7 +852,7 @@
 def kernel(
     lengths, inputs, cotangent, wq_src, wk_src, wv_src, wup_src, wdn_src, wout_src, pk_src, pv_src,
     v0, v1, v2, v3, v4, v5, v6, v7, v8,
-    out_y, out_dx, got_qkv, got_up, got_dn, got_out, got_prefix, got_rows, got_bias,
+    out_y, out_dx, out_q, out_k, out_v, out_o, out_up, out_dn, out_pk, out_pv, got_rows, got_bias,
     ag_recv, ag_sib, ag_send, rs_recv, rs_send,
     wsend, wown, wtwin, wrelay, psem, xsem, osend, orecv, tsend, trecv, gsend, grecv, rsem,
     raw_qkv, raw_up, pack_qkv, pack_up, vrows, u0, u1, u2, u3, u4, u5, u6, u7, u8,
@@ -866,6 +865,7 @@
     dfs, dcb, delta, dqt, dkacc, dvacc, dqkv, dqkvt,
     rowacc, biasacc, g_qkv, g_up, g_dn, g_out, g_prefix,
     t_qkv, t_up, t_dn, t_out, t_prefix,
+    got_qkv, got_up, got_dn, got_out, got_prefix,
 ):
     place = Place()
     x, t, cube, core, tau = place.x, place.t, place.cube, place.core, place.tau
@@ -1112,8 +1112,8 @@
             gather_x.pump.go(1)
             relay_out(0)
             gather_x.stage(1)
+            gather_x.pump.go(len(gather_x.pump.waiting))
             relay_blocks(1, 0)
-            gather_x.pump.go(len(gather_x.pump.waiting))
             gather_x.stage(2)
             relay_down(0)
             d_start()
@@ -1159,7 +1159,7 @@
 
         give_out, give_down = slice_pushes()
         scatter_o = scatter(RS_O)
-        scatter_o.pump = Pump(9)
+        scatter_o.pump = Pump(5)
         scatter_o.pump.add(
             [second_layer(start) for start in (*spread_pushes(0), give_out, give_down, *spread_pushes(1))]
         )
@@ -1181,6 +1181,7 @@
         pl.when(l == 0)(lambda: weights_in(2, 0))
         pl.when(l == 1)(lambda: weights_in(2, 1))
         scatter_o.run(attend)
+        scatter_o.pump.go(len(scatter_o.pump.waiting))
         attended = scatter_o.finish() + param[l, 0:1]
         normal = norm_forward(
             xg[l, own_rows].astype(F32) + attended,
@@ -1408,7 +1409,7 @@
         def older(start):
             return lambda: pl.when(l == 0)(start)
 
-        pump = Pump()
+        pump = Pump(1)
         twins = [*twin_chunks(3, l), *twin_chunks(1, l)]
         olds = [older(start) for kind in (3, 1, 4, 0, 2) for start in owner_pushes(kind, 1)]
         for k in range(17):
@@ -1508,8 +1509,36 @@
     for kind, out in ((0, out_y), (1, out_dx)):
         for m in range(2):
             bytes_of(out.at[m], orecv.at[kind, m]).wait()
-    for kind, ref in enumerate((got_qkv, got_up, got_prefix, got_dn, got_out, got_rows, got_bias)):
+
+    def landed(kind):
+        ref = (got_qkv, got_up, got_prefix, got_dn, got_out, got_rows, got_bias)[kind]
         bytes_of(ref, grecv.at[kind]).wait()
+
+    landed(3)
+    out_dn[0] = got_dn[...].astype(F32)
+    landed(1)
+    for side in range(2):
+        for rest in range(8):
+            for zhi in range(2):
+                start = (zhi * 8 + rest) * 256 + side * 128
+                part = got_up[side * 8 + rest, :, zhi * 128 : (zhi + 1) * 128]
+                out_up[0, :, start : start + 128] = part.astype(F32)
+    landed(4)
+    out_o[0] = got_out[...].astype(F32)
+
+    def heads_together(got, outs):
+        for h in range(8):
+            pair = [got[2 * h].astype(F32), got[2 * h + 1].astype(F32)]
+            for i, out in enumerate(outs):
+                sides = [value[:, i * 64 : (i + 1) * 64] for value in pair]
+                out[0, :, h * 128 : (h + 1) * 128] = jnp.concatenate(sides, axis=1)
+
+    landed(2)
+    heads_together(got_prefix, (out_pk, out_pv))
+    landed(0)
+    heads_together(got_qkv, (out_q, out_k, out_v))
+    landed(5)
+    landed(6)
 
 
 def cube_local(
@@ -1535,12 +1564,13 @@
         kernel,
         out_shape=(
             shape((2, ROWS, width), BF16), shape((2, ROWS, width), BF16),
-            shape((16, ROWS, 256), BF16), shape((16, ROWS, 256), BF16),
-            shape((hidden, width), BF16), shape((ROWS, width), BF16),
-            shape((16, prefix, 128), BF16), shape((32, 8, 128), F32), shape((4, 8, hidden), F32),
+            shape((1, rows, width), F32), shape((1, rows, width), F32), shape((1, rows, width), F32),
+            shape((1, rows, width), F32), shape((1, rows, 4 * width), F32), shape((1, hidden, width), F32),
+            shape((1, prefix, width), F32), shape((1, prefix, width), F32),
+            shape((32, 8, 128), F32), shape((4, 8, hidden), F32),
         ),
         in_specs=[smem] + [anywhere] * 19,
-        out_specs=[anywhere] * 9,
+        out_specs=[anywhere] * 2 + [pl.BlockSpec(memory_space=pltpu.VMEM)] * 8 + [anywhere] * 2,
         scratch_shapes=[
             dma((4, 8, PIECES)), dma((4, 8, PIECES)), dma((3, 8, PIECES)), dma((4, 2, 8)), dma((2, 8)),
             dma((4,)), dma((4, 2, 8)), dma((4, 2)), dma((4, 2)), dma((3, 2)), dma((8,)),
@@ -1568,6 +1598,8 @@
             V((L, ROWS, width), BF16), V((L, prefix, 128), BF16),
             V((L, width // 2, 256), BF16), V((L, width // 2, 256), BF16), V((L, hidden // 2, width), BF16),
             V((L, ROWS, width), BF16), V((L, prefix // 2, 128), BF16),
+            V((16, ROWS, 256), BF16), V((16, ROWS, 256), BF16), V((hidden, width), BF16), V((ROWS, width), BF16),
+            V((16, prefix, 128), BF16),
         ],
         compiler_params=pltpu.CompilerParams(
             collective_id=0, has_side_effects=True, vmem_limit_bytes=60 * 2**20
@@ -1576,12 +1608,7 @@
         lengths, inputs, cotangent, w_query, w_key, w_value, w_up, w_down, w_out, prefix_keys, prefix_values,
         b_out, norm1_gain, norm1_shift, b_down, norm2_gain, norm2_shift, b_query, b_value, b_up,
     )
-    out_y, out_dx, got_qkv, got_up, got_dn, got_out, got_prefix, got_rows, got_bias = results
-
-    def side_by_side(value):
-        return value.astype(F32).transpose(1, 0, 2).reshape(1, value.shape[1], -1)
-
-    up = got_up.reshape(2, 8, rows, 2, 128).transpose(2, 3, 1, 0, 4).astype(F32)
+    out_y, out_dx, out_q, out_k, out_v, out_o, out_up, out_dn, out_pk, out_pv, got_rows, got_bias = results
     row_sum = lax.dynamic_slice_in_dim(jnp.sum(got_rows, axis=0), (t % 2) * 64, 64, 1)
     side = t // 8
     bias_up = (got_bias[:2, 1] + got_bias[2:, 1]).reshape(2, 2, 128)
@@ -1590,23 +1617,23 @@
     return (
         out_y[None],
         out_dx[None],
-        side_by_side(got_qkv[:, :, :64]),
+        out_q,
         bias_qkv[:, 0:64],
-        side_by_side(got_qkv[:, :, 64:128]),
-        side_by_side(got_qkv[:, :, 128:192]),
+        out_k,
+        out_v,
         bias_qkv[:, 128:192],
-        got_out[None].astype(F32),
+        out_o,
         row_sum[2:3],
         row_sum[0:1],
         row_sum[1:2],
-        up.reshape(1, rows, -1),
+        out_up,
         bias_up,
-        got_dn[None].astype(F32),
+        out_dn,
         row_sum[5:6],
         row_sum[3:4],
         row_sum[4:5],
-        side_by_side(got_prefix[:, :, :64]),
-        side_by_side(got_prefix[:, :, 64:]),
+        out_pk,
+        out_pv,
     )
 
 

time: 389 us -> 374 us (0.961); the launches traced: 388 us -> 368 us
  Pallas kernels: 370 us -> 355 us
    pallas_call x1, Pallas kernels: 370 us -> 355 us  [cube_local(): pl.pallas_call(kernel, out_shape=(shape((2, ROWS, width), BF16), shape((2...]
    reshape x13 -> x0, local copies, waits for them, and re-layouts: 9.07 us -> none  [the longest x10 5.94 us: side_by_side(): return value.astype(F32).transpose(1, 0, 2).reshape(1, value.shape[1], -1)]
    unnamed x12 -> x28, local copies, waits for them, and re-layouts: 2.23 us -> 10 us
where the time goes in v3:
time: 374 us; the launch traced here: 368 us
  Pallas kernels  355 us (95%)
  local copies, waits for them, and re-layouts  11.2 us (3%)
    pallas_call x1, Pallas kernels, cube_local(): pl.pallas_call(kernel, out_shape=(shape((2, ROWS, width), BF16), shape((2...  355 us
    unnamed x28, local copies, waits for them, and re-layouts  10 us

profile of v3, /device:TPU:0, one launch (start us, length us, event | category | flops | bytes accessed | tf_op | source)
XLA Modules:
  0.0 368.3 jit_solution(8819787635579190559)
XLA Ops:
  0.7 354.6 %shard_map.339 = (bf16[2,64,1024]{2,1,0:T(8,128)(2,1)}, bf16[2,64,1024]{2,1,0:T(8,128)(2,1)}, f32[1,64,1024]{2,1,0:T(8,128)}, f32[1,64,1024]{2,1,0:T(8,128)}, f3...) custom-call(s32[2,8]{1,0:T(2,128)} %lengths.1, ...), custom_call_target="tpu_custom_call" | custom-call | tf_op jit(solution)/shard_map/pallas_call | solution.py:1563
  355.3 0.9 reduce_sum.9
  356.3 0.1 constant_dynamic-slice_fusion
  356.3 0.8 slice_add_fusion
  357.1 0.6 dynamic-slice_bitcast_fusion
  357.7 0.5 fusion.1
  358.2 0.0 copy-start.8
  358.2 0.0 copy-start.7
  358.2 1.7 copy.49
  360.0 0.0 copy-done.8
  360.0 0.0 copy-start.6
  360.0 0.0 copy-start.5
  360.0 0.7 copy.50
  360.7 0.0 copy-done.7
  360.7 0.0 copy-start.1
  360.7 0.7 copy.51
  361.4 0.0 copy-done.6
  361.4 0.7 copy.52
  362.1 0.0 copy-done.5
  362.1 0.0 copy-start.4
  362.1 0.7 copy.53
  362.8 0.3 copy-done.4
  363.1 0.7 copy.54
  363.9 0.0 copy-done.1
  363.9 0.0 copy-start
  363.9 1.0 copy.55
  364.8 0.6 copy-done
  365.5 0.0 copy-start.3
  365.5 1.0 copy.56
  366.4 0.1 copy-done.3
  366.5 0.0 copy-start.2
  366.6 0.7 copy.57
  367.3 0.3 copy-done.2
  367.6 0.7 copy.58
  (1 shorter events, 0.0 us)
Async XLA Ops:
  358.2 1.7 copy-start.8
  358.2 2.4 copy-start.7
  360.0 1.4 copy-start.6
  360.0 2.1 copy-start.5
  360.7 3.2 copy-start.1
  362.1 1.0 copy-start.4
  363.9 1.6 copy-start
  365.5 1.1 copy-start.3
  366.5 1.0 copy-start.2

commit v4 on v3

--- a/solution.py
+++ b/solution.py
@@ -1483,11 +1483,6 @@
         lax.fori_loop(this_half * 2, this_half * 2 + 2, qkv_tile, 0)
         pump.go(len(pump.waiting))
 
-        @pl.when(l == 0)
-        def _():
-            for kind in (3, 1):
-                owner_start(kind, 0)
-
         dstage[l] = (own_a[...] + scatter_x.finish()).astype(BF16)
         is_self, here, there = result_out(dstage.at[l], out_dx, 1, l)
         pl.when(is_self)(here.start)
@@ -1495,7 +1490,7 @@
         return carry
 
     lax.fori_loop(0, 2, backward_layer, 0)
-    for kind in (2, 4, 0):
+    for kind in (3, 1, 2, 4, 0):
         owner_start(kind, 0)
 
     x_sent()

time: 374 us -> 374 us (level)
  no operation moved by 1% of the time
where the time goes in v4:
time: 374 us; the launch traced here: 368 us
  Pallas kernels  355 us (95%)
  local copies, waits for them, and re-layouts  11.2 us (3%)
    pallas_call x1, Pallas kernels, cube_local(): pl.pallas_call(kernel, out_shape=(shape((2, ROWS, width), BF16), shape((2...  355 us
    unnamed x28, local copies, waits for them, and re-layouts  10 us

profile of v4, /device:TPU:0, one launch (start us, length us, event | category | flops | bytes accessed | tf_op | source)
XLA Modules:
  0.0 368.3 jit_solution(12576695450080972980)
XLA Ops:
  0.7 354.6 %shard_map.339 = (bf16[2,64,1024]{2,1,0:T(8,128)(2,1)}, bf16[2,64,1024]{2,1,0:T(8,128)(2,1)}, f32[1,64,1024]{2,1,0:T(8,128)}, f32[1,64,1024]{2,1,0:T(8,128)}, f3...) custom-call(s32[2,8]{1,0:T(2,128)} %lengths.1, ...), custom_call_target="tpu_custom_call" | custom-call | tf_op jit(solution)/shard_map/pallas_call | solution.py:1558
  355.3 0.9 reduce_sum.9
  356.2 0.1 constant_dynamic-slice_fusion
  356.3 0.8 slice_add_fusion
  357.1 0.6 dynamic-slice_bitcast_fusion
  357.7 0.5 fusion.1
  358.2 0.0 copy-start.8
  358.2 0.0 copy-start.7
  358.2 1.7 copy.49
  360.0 0.0 copy-done.8
  360.0 0.0 copy-start.6
  360.0 0.0 copy-start.5
  360.0 0.7 copy.50
  360.7 0.0 copy-done.7
  360.7 0.0 copy-start.1
  360.7 0.7 copy.51
  361.4 0.0 copy-done.6
  361.4 0.7 copy.52
  362.1 0.0 copy-done.5
  362.1 0.0 copy-start.4
  362.1 0.7 copy.53
  362.8 0.3 copy-done.4
  363.1 0.7 copy.54
  363.8 0.0 copy-done.1
  363.8 0.0 copy-start
  363.8 1.0 copy.55
  364.8 0.6 copy-done
  365.4 0.0 copy-start.3
  365.5 1.0 copy.56
  366.4 0.1 copy-done.3
  366.5 0.0 copy-start.2
  366.5 0.7 copy.57
  367.2 0.3 copy-done.2
  367.6 0.7 copy.58
  (1 shorter events, 0.0 us)
Async XLA Ops:
  358.2 1.7 copy-start.8
  358.2 2.4 copy-start.7
  360.0 1.4 copy-start.6
  360.0 2.1 copy-start.5
  360.7 3.2 copy-start.1
  362.1 1.0 copy-start.4
  363.8 1.6 copy-start
  365.4 1.1 copy-start.3
  366.5 1.0 copy-start.2
